TPU v7x, 32 devices: a whole 2x2x4 slice. The times are simulated.
32 devices in a mesh: groups: 2 (over y), sector: 16 (over z, x, core).
Axes of the slice: x: 2, y: 2, z: 4, core: 2. Of those that a mesh axis runs over, the one named last changes fastest.
Arguments:
- wavefunction: float32 [32, 256, 256], P(('groups', 'sector')), parts along dimension 0, may hold values from -1200 to 1200
- sector_dims: int32 [32, 2], P(('groups', 'sector')), parts along dimension 0, may hold values from 64 to 256
- left_env: bfloat16 [32, 26, 256, 256], P(('groups', 'sector')), parts along dimension 0, may hold values from -2 to 2
- right_env: bfloat16 [32, 26, 256, 256], P(('groups', 'sector')), parts along dimension 0, may hold values from -2 to 2
Outputs:
- first_image: float32 [32, 256, 256], P(('groups', 'sector')), parts along dimension 0
- second_image: float32 [32, 256, 256], P(('groups', 'sector')), parts along dimension 0
There are 2 independent parts, one for each index of `groups`. A program takes and returns all parts, laid end to end along the dimension named above; each array names one. Nothing has to cross between parts.
All inputs are finite; a program needn't handle non-finite values.
Results may differ from a plain program's by a relative error of at most 0.009.
Values may be sent and summed in bfloat16 or wider, within the bound.
No kernel may reach another device: no remote copies, remote signals or barrier semaphores. Data moves between devices by JAX's collectives and lax.ppermute only.
A program may use at most 64 MiB of HBM per device.

v0:
```python
import jax
import jax.numpy as jnp
from jax import lax
from jax.sharding import PartitionSpec as P

QD = 8


def shifted(x, axis, by):
    size = lax.axis_size(axis)
    pairs = [(i, i + by) for i in range(size) if 0 <= i + by < size]
    return lax.ppermute(x, axis, pairs)


def apply_operator(vector, left_env, right_env, live_mask):
    position = lax.axis_index("sector")
    column = position % QD
    below = shifted(vector, "sector", 1)
    above = shifted(vector, "sector", -1)
    zero_block = jnp.zeros_like(vector)
    below = jnp.where(column >= 1, below, zero_block)
    above = jnp.where(column <= QD - 2, above, zero_block)
    lower_row = shifted(vector, "sector", QD)
    upper_row = shifted(vector, "sector", -QD)
    sources = (vector, below, above, lower_row, upper_row)
    width_terms = (right_env.shape[1] - 2) // 4
    bounds = [0, 2, 2 + width_terms, 2 + 2 * width_terms, 2 + 3 * width_terms, 2 + 4 * width_terms]
    pieces = []
    for number in range(5):
        partial_value = jnp.einsum(
            "ab,kcb->kac",
            sources[number][0],
            right_env[0, bounds[number] : bounds[number + 1]],
            preferred_element_type=jnp.float32,
        )
        pieces.append(partial_value.astype(jnp.bfloat16))
    stacked = jnp.concatenate(pieces, axis=0)
    image = lax.dot_general(
        left_env[0], stacked, (((0, 2), (0, 1)), ((), ())), preferred_element_type=jnp.float32
    )
    return (image * live_mask)[None]


def body(wavefunction, sector_dims, left_env, right_env):
    block_size = wavefunction.shape[1]
    rows_index = jnp.arange(block_size, dtype=jnp.int32)
    row_ok = rows_index < sector_dims[0, 0]
    col_ok = rows_index < sector_dims[0, 1]
    live_mask = (row_ok[:, None] & col_ok[None, :]).astype(jnp.float32)
    cell_count = jnp.float32(lax.axis_size("sector") * block_size * block_size)
    local_norm = jnp.sum(live_mask * wavefunction[0] * wavefunction[0])
    start_norm = lax.psum(local_norm, "sector")
    first_vector = (
        live_mask[None] * wavefunction * lax.rsqrt(start_norm / cell_count + 1e-06)
    ).astype(jnp.bfloat16)
    first_image = apply_operator(first_vector, left_env, right_env, live_mask)
    first_wide = first_vector.astype(jnp.float32)
    cross_sum, vector_sum = lax.psum(
        (jnp.sum(first_wide * first_image), jnp.sum(first_wide * first_wide)), "sector"
    )
    rayleigh = cross_sum / vector_sum
    residual_field = first_image - rayleigh * first_wide
    residual_norm = lax.psum(jnp.sum(residual_field * residual_field), "sector")
    second_vector = (residual_field * lax.rsqrt(residual_norm / cell_count + 1e-06)).astype(
        jnp.bfloat16
    )
    second_image = apply_operator(second_vector, left_env, right_env, live_mask)
    return (first_image, second_image)


def solution(mesh):
    placed = (
        P(("groups", "sector"), None, None),
        P(("groups", "sector"), None),
        P(("groups", "sector"), None, None, None),
        P(("groups", "sector"), None, None, None),
    )
    return jax.shard_map(
        body,
        mesh=mesh,
        in_specs=placed,
        out_specs=(P(("groups", "sector"), None, None), P(("groups", "sector"), None, None)),
        check_vma=False,
    )
```

profile of v0, /device:TPU:0, one launch (start us, length us, event | category | flops | bytes accessed | tf_op | source)
XLA Modules:
  0.0 152.7 jit_solution(15397765923775514232)
XLA Ops:
  2.1 1.8 %copy.6 = f32[1,256,256]{1,2,0:T(8,128)} copy(f32[1,256,256]{2,1,0:T(8,128)} %param.4) | data formatting | bytes 524288 | tf_op args[0]
  5.2 1.7 %fusion.62 = f32[]{:T(128)} fusion(f32[1,256,256]{1,2,0:T(8,128)} %copy.6, pred[256]{0:T(512)(128)(4,1)S(1)} %get-tuple-element.12, pred[256]{0:T(512)(128)(4,1)S(1)} %get-tuple-element.11), kind=kLoop, calls=%fused_computation.64 | loop fusion | flops 262143 | bytes 262660 | tf_op jit(solution)/shard_map/reduce_sum | solution.py:51
  6.9 35.5 %psum.28 = f32[]{:T(128)} all-reduce(f32[]{:T(128)} %fusion.62), channel_id=1, replica_groups=mesh['groups'=2,'sector'=16] {'sector'}, use_global_device_ids=true, to_apply=%region_1.0 | all-reduce | flops 1 | bytes 8 | tf_op jit(solution)/shard_map/psum | solution.py:52
  44.2 1.9 %collective-permute-start = (bf16[1,256,256]{1,2,0:T(8,128)(2,1)S(1)}, bf16[1,256,256]{1,2,0:T(8,128)(2,1)}, u32[]{:S(2)}, u32[]{:S(2)}) collective-permute-start(bf16[1,256,256]{1,2,0:T(8,128)(2,1)S(1)} %multiply_convert_fusion.1), channel_id=1, source_target_pairs={{0,1},{1,2},{2,3},{3,4},{4,5},{5,6},{6,7},{7,8},{8,9},{9,10},{10,1... | collective-permute-start | bytes 393224 | tf_op jit(solution)/shard_map/ppermute | solution.py:12
  47.4 2.0 %collective-permute-start.2 = (bf16[1,256,256]{1,2,0:T(8,128)(2,1)S(1)}, bf16[1,256,256]{1,2,0:T(8,128)(2,1)}, u32[]{:S(2)}, u32[]{:S(2)}) collective-permute-start(bf16[1,256,256]{1,2,0:T(8,128)(2,1)S(1)} %multiply_convert_fusion.1), channel_id=1, source_target_pairs={{0,8},{1,9},{2,10},{3,11},{4,12},{5,13},{6,14},{7,15},{16,24},{17,... | collective-permute-start | bytes 393224 | tf_op jit(solution)/shard_map/ppermute | solution.py:12
  51.8 1.5 fusion.5
  53.4 1.6 %fusion.7 = bf16[26,256,256]{1,2,0:T(8,128)(2,1)S(1)} fusion(bf16[26,256,256]{1,2,0:T(8,128)(2,1)S(1)} %fusion.5, bf16[1,26,256,256]{3,2,1,0:T(8,128)(2,1)} %param.7, bf16[1,256,256]{1,2,0:T(8,128)(2,1)} %collective-permute-done.1, pred[]{:T(512)S(6)} %le.4), kind=kOutput, calls=%fused_computation.15 | convolution fusion | flops 201785344 | bytes 1703937 | tf_op jit(solution)/shard_map/ab,kcb->kac/dot_general | solution.py:30
  55.0 1.6 %fusion.9 = bf16[26,256,256]{1,2,0:T(8,128)(2,1)S(1)} fusion(bf16[26,256,256]{1,2,0:T(8,128)(2,1)S(1)} %fusion.7, bf16[1,26,256,256]{3,2,1,0:T(8,128)(2,1)} %param.7, bf16[1,256,256]{1,2,0:T(8,128)(2,1)} %collective-permute-done.2), kind=kOutput, calls=%fused_computation.17 | convolution fusion | flops 201719808 | bytes 1703936 | tf_op jit(solution)/shard_map/ab,kcb->kac/dot_general | solution.py:30
  56.5 2.6 %collective-permute-done.3 = bf16[1,256,256]{1,2,0:T(8,128)(2,1)} collective-permute-done((bf16[1,256,256]{1,2,0:T(8,128)(2,1)S(1)}, bf16[1,256,256]{1,2,0:T(8,128)(2,1)}, u32[]{:S(2)}, u32[]{:S(2)}) %collective-permute-start.3) | collective-permute-done | bytes 131104 | tf_op jit(solution)/shard_map/ppermute | solution.py:12
  59.1 1.6 %fusion.11 = bf16[26,256,256]{1,2,0:T(8,128)(2,1)S(1)} fusion(bf16[26,256,256]{1,2,0:T(8,128)(2,1)S(1)} %fusion.9, bf16[1,26,256,256]{3,2,1,0:T(8,128)(2,1)} %param.7, bf16[1,256,256]{1,2,0:T(8,128)(2,1)} %collective-permute-done.3), kind=kOutput, calls=%fused_computation.19 | convolution fusion | flops 201719808 | bytes 1703936 | tf_op jit(solution)/shard_map/ab,kcb->kac/dot_general | solution.py:30
  60.7 2.4 %fusion.60 = (f32[]{:T(128)}, f32[]{:T(128)}, f32[1,256,256]{1,2,0:T(8,128)}) fusion(bf16[1,256,256]{1,2,0:T(8,128)(2,1)S(1)} %multiply_convert_fusion.1, bf16[26,256,256]{1,2,0:T(8,128)(2,1)S(1)} %fusion.11, bf16[1,26,256,256]{3,2,1,0:T(8,128)(2,1)S(1)} %copy-done, pred[256]{0:T(512)(128)(4,1)S(1)} %get-tuple-element.11, ...), kind=kOutput, calls=%fused_computation.62 | convolution fusion | flops 872873984 | bytes 7209480 | tf_op jit(solution)/shard_map/dot_general | solution.py:38
  63.2 33.0 %all-reduce = (f32[]{:T(128)}, f32[]{:T(128)}) all-reduce(f32[]{:T(128)} %get-tuple-element.5, f32[]{:T(128)} %get-tuple-element.4), channel_id=1, replica_groups=mesh['groups'=2,'sector'=16] {'sector'}, use_global_device_ids=true, to_apply=%region_3.4 | all-reduce | flops 2 | bytes 16 | tf_op jit(solution)/shard_map/psum | solution.py:58
  97.5 1.8 %multiply_reduce_fusion = f32[]{:T(128)} fusion(f32[1,256,256]{1,2,0:T(8,128)} %get-tuple-element.10, f32[]{:T(128)S(6)} %div.10, f32[]{:T(128)S(6)} %rsqrt.6, f32[1,256,256]{1,2,0:T(8,128)} %copy.6, pred[256]{0:T(512)(128)(4,1)S(1)} %get-tuple-element.11, pred[256]{0:T(512)(128)(4,1)S(1)} %get-tuple-element.12), kind=kLoop, calls=%fused_computation.68 | loop fusion | flops 589823 | bytes 524812 | tf_op jit(solution)/shard_map/reduce_sum | solution.py:63
  99.3 30.1 %psum.31 = f32[]{:T(128)} all-reduce(f32[]{:T(128)} %multiply_reduce_fusion), channel_id=1, replica_groups=mesh['groups'=2,'sector'=16] {'sector'}, use_global_device_ids=true, to_apply=%region_7.8 | all-reduce | flops 1 | bytes 8 | tf_op jit(solution)/shard_map/psum | solution.py:63
  131.2 2.4 %collective-permute-start.4 = (bf16[1,256,256]{1,2,0:T(8,128)(2,1)S(1)}, bf16[1,256,256]{1,2,0:T(8,128)(2,1)}, u32[]{:S(2)}, u32[]{:S(2)}) collective-permute-start(bf16[1,256,256]{1,2,0:T(8,128)(2,1)S(1)} %multiply_convert_fusion), channel_id=1, source_target_pairs={{0,1},{1,2},{2,3},{3,4},{4,5},{5,6},{6,7},{7,8},{8,9},{9,10},{10,1... | collective-permute-start | bytes 393224 | tf_op jit(solution)/shard_map/ppermute | solution.py:12
  135.0 1.9 %collective-permute-start.6 = (bf16[1,256,256]{1,2,0:T(8,128)(2,1)S(1)}, bf16[1,256,256]{1,2,0:T(8,128)(2,1)}, u32[]{:S(2)}, u32[]{:S(2)}) collective-permute-start(bf16[1,256,256]{1,2,0:T(8,128)(2,1)S(1)} %multiply_convert_fusion), channel_id=1, source_target_pairs={{0,8},{1,9},{2,10},{3,11},{4,12},{5,13},{6,14},{7,15},{16,24},{17,... | collective-permute-start | bytes 393224 | tf_op jit(solution)/shard_map/ppermute | solution.py:12
  138.2 1.8 %copy.8 = f32[1,256,256]{2,1,0:T(8,128)} copy(f32[1,256,256]{1,2,0:T(8,128)} %get-tuple-element.10) | data formatting | bytes 524288
  141.2 1.5 fusion.13
  142.7 1.6 %fusion.15 = bf16[26,256,256]{1,2,0:T(8,128)(2,1)S(1)} fusion(bf16[26,256,256]{1,2,0:T(8,128)(2,1)S(1)} %fusion.13, bf16[1,26,256,256]{3,2,1,0:T(8,128)(2,1)} %param.7, bf16[1,256,256]{1,2,0:T(8,128)(2,1)} %collective-permute-done.5, pred[]{:T(512)S(6)} %le.4), kind=kOutput, calls=%fused_computation.23 | convolution fusion | flops 201785344 | bytes 1703937 | tf_op jit(solution)/shard_map/ab,kcb->kac/dot_general | solution.py:30
  144.3 1.6 %fusion.17 = bf16[26,256,256]{1,2,0:T(8,128)(2,1)S(1)} fusion(bf16[26,256,256]{1,2,0:T(8,128)(2,1)S(1)} %fusion.15, bf16[1,26,256,256]{3,2,1,0:T(8,128)(2,1)} %param.7, bf16[1,256,256]{1,2,0:T(8,128)(2,1)} %collective-permute-done.6), kind=kOutput, calls=%fused_computation.25 | convolution fusion | flops 201719808 | bytes 1703936 | tf_op jit(solution)/shard_map/ab,kcb->kac/dot_general | solution.py:30
  145.9 1.6 %collective-permute-done.7 = bf16[1,256,256]{1,2,0:T(8,128)(2,1)} collective-permute-done((bf16[1,256,256]{1,2,0:T(8,128)(2,1)S(1)}, bf16[1,256,256]{1,2,0:T(8,128)(2,1)}, u32[]{:S(2)}, u32[]{:S(2)}) %collective-permute-start.7) | collective-permute-done | bytes 131104 | tf_op jit(solution)/shard_map/ppermute | solution.py:12
  147.5 1.6 %fusion.19 = bf16[26,256,256]{1,2,0:T(8,128)(2,1)S(1)} fusion(bf16[26,256,256]{1,2,0:T(8,128)(2,1)S(1)} %fusion.17, bf16[1,26,256,256]{3,2,1,0:T(8,128)(2,1)} %param.7, bf16[1,256,256]{1,2,0:T(8,128)(2,1)} %collective-permute-done.7), kind=kOutput, calls=%fused_computation.27 | convolution fusion | flops 201719808 | bytes 1703936 | tf_op jit(solution)/shard_map/ab,kcb->kac/dot_general | solution.py:30
  149.1 1.8 %fusion.33 = f32[1,256,256]{1,2,0:T(8,128)} fusion(bf16[26,256,256]{1,2,0:T(8,128)(2,1)S(1)} %fusion.19, bf16[1,26,256,256]{3,2,1,0:T(8,128)(2,1)S(1)} %copy-done, pred[256]{0:T(512)(128)(4,1)S(1)} %get-tuple-element.12, pred[256]{0:T(512)(128)(4,1)S(1)} %get-tuple-element.11), kind=kOutput, calls=%fused_computation.37 | convolution fusion | flops 872546304 | bytes 7078400 | tf_op jit(solution)/shard_map/dot_general | solution.py:38
  150.9 1.8 %copy.9 = f32[1,256,256]{2,1,0:T(8,128)} copy(f32[1,256,256]{1,2,0:T(8,128)} %fusion.33) | data formatting | bytes 524288
  (18 shorter events, 12.5 us)
Async XLA Ops:
  0.6 60.1 %copy-start = (bf16[1,26,256,256]{3,2,1,0:T(8,128)(2,1)S(1)}, bf16[1,26,256,256]{3,2,1,0:T(8,128)(2,1)}, u32[]{:S(2)}) copy-start(bf16[1,26,256,256]{3,2,1,0:T(8,128)(2,1)} %param.6) | copy-start | bytes 10223620
  44.2 7.7 %collective-permute-start = (bf16[1,256,256]{1,2,0:T(8,128)(2,1)S(1)}, bf16[1,256,256]{1,2,0:T(8,128)(2,1)}, u32[]{:S(2)}, u32[]{:S(2)}) collective-permute-start(bf16[1,256,256]{1,2,0:T(8,128)(2,1)S(1)} %multiply_convert_fusion.1), channel_id=1, source_target_pairs={{0,1},{1,2},{2,3},{3,4},{4,5},{5,6},{6,7},{7,8},{8,9},{9,10},{10,1... | collective-permute-start | bytes 393224 | tf_op jit(solution)/shard_map/ppermute | solution.py:12
  46.1 7.3 %collective-permute-start.1 = (bf16[1,256,256]{1,2,0:T(8,128)(2,1)S(1)}, bf16[1,256,256]{1,2,0:T(8,128)(2,1)}, u32[]{:S(2)}, u32[]{:S(2)}) collective-permute-start(bf16[1,256,256]{1,2,0:T(8,128)(2,1)S(1)} %multiply_convert_fusion.1), channel_id=1, source_target_pairs={{1,0},{2,1},{3,2},{4,3},{5,4},{6,5},{7,6},{8,7},{9,8},{10,9},{11,1... | collective-permute-start | bytes 393224 | tf_op jit(solution)/shard_map/ppermute | solution.py:12
  47.4 7.6 %collective-permute-start.2 = (bf16[1,256,256]{1,2,0:T(8,128)(2,1)S(1)}, bf16[1,256,256]{1,2,0:T(8,128)(2,1)}, u32[]{:S(2)}, u32[]{:S(2)}) collective-permute-start(bf16[1,256,256]{1,2,0:T(8,128)(2,1)S(1)} %multiply_convert_fusion.1), channel_id=1, source_target_pairs={{0,8},{1,9},{2,10},{3,11},{4,12},{5,13},{6,14},{7,15},{16,24},{17,... | collective-permute-start | bytes 393224 | tf_op jit(solution)/shard_map/ppermute | solution.py:12
  49.3 9.8 %collective-permute-start.3 = (bf16[1,256,256]{1,2,0:T(8,128)(2,1)S(1)}, bf16[1,256,256]{1,2,0:T(8,128)(2,1)}, u32[]{:S(2)}, u32[]{:S(2)}) collective-permute-start(bf16[1,256,256]{1,2,0:T(8,128)(2,1)S(1)} %multiply_convert_fusion.1), channel_id=1, source_target_pairs={{8,0},{9,1},{10,2},{11,3},{12,4},{13,5},{14,6},{15,7},{24,16},{25,... | collective-permute-start | bytes 393224 | tf_op jit(solution)/shard_map/ppermute | solution.py:12
  131.2 9.9 %collective-permute-start.4 = (bf16[1,256,256]{1,2,0:T(8,128)(2,1)S(1)}, bf16[1,256,256]{1,2,0:T(8,128)(2,1)}, u32[]{:S(2)}, u32[]{:S(2)}) collective-permute-start(bf16[1,256,256]{1,2,0:T(8,128)(2,1)S(1)} %multiply_convert_fusion), channel_id=1, source_target_pairs={{0,1},{1,2},{2,3},{3,4},{4,5},{5,6},{6,7},{7,8},{8,9},{9,10},{10,1... | collective-permute-start | bytes 393224 | tf_op jit(solution)/shard_map/ppermute | solution.py:12
  133.7 9.0 %collective-permute-start.5 = (bf16[1,256,256]{1,2,0:T(8,128)(2,1)S(1)}, bf16[1,256,256]{1,2,0:T(8,128)(2,1)}, u32[]{:S(2)}, u32[]{:S(2)}) collective-permute-start(bf16[1,256,256]{1,2,0:T(8,128)(2,1)S(1)} %multiply_convert_fusion), channel_id=1, source_target_pairs={{1,0},{2,1},{3,2},{4,3},{5,4},{6,5},{7,6},{8,7},{9,8},{10,9},{11,1... | collective-permute-start | bytes 393224 | tf_op jit(solution)/shard_map/ppermute | solution.py:12
  135.0 9.3 %collective-permute-start.6 = (bf16[1,256,256]{1,2,0:T(8,128)(2,1)S(1)}, bf16[1,256,256]{1,2,0:T(8,128)(2,1)}, u32[]{:S(2)}, u32[]{:S(2)}) collective-permute-start(bf16[1,256,256]{1,2,0:T(8,128)(2,1)S(1)} %multiply_convert_fusion), channel_id=1, source_target_pairs={{0,8},{1,9},{2,10},{3,11},{4,12},{5,13},{6,14},{7,15},{16,24},{17,... | collective-permute-start | bytes 393224 | tf_op jit(solution)/shard_map/ppermute | solution.py:12
  136.9 10.6 %collective-permute-start.7 = (bf16[1,256,256]{1,2,0:T(8,128)(2,1)S(1)}, bf16[1,256,256]{1,2,0:T(8,128)(2,1)}, u32[]{:S(2)}, u32[]{:S(2)}) collective-permute-start(bf16[1,256,256]{1,2,0:T(8,128)(2,1)S(1)} %multiply_convert_fusion), channel_id=1, source_target_pairs={{8,0},{9,1},{10,2},{11,3},{12,4},{13,5},{14,6},{15,7},{24,16},{25,... | collective-permute-start | bytes 393224 | tf_op jit(solution)/shard_map/ppermute | solution.py:12
where the time goes:
time: 153 us
  blocking collectives  98.6 us (64%)
  matrix products  19.1 us (12%)
  starting transfers between devices  13.4 us (9%)
  other arithmetic  7.04 us (5%)
  local copies, waits for them, and re-layouts  6.78 us (4%)
  waiting for transfers between devices  4.22 us (3%)
  between operations  3.56 us (2%)
    psum x1, blocking collectives, body(): start_norm = lax.psum(local_norm, 'sector')  35.5 us
    psum x1, blocking collectives, body(): lax.psum((jnp.sum(first_wide * first_image), jnp.sum(first_wide * first_w...  33 us
    psum x1, blocking collectives, body(): residual_norm = lax.psum(jnp.sum(residual_field * residual_field), 'sector')  30.1 us
    dot_general x10, matrix products, apply_operator(): jnp.einsum('ab,kcb->kac', sources[number][0], right_env[0, bounds[number]...  14.8 us
    ppermute x8, starting transfers between devices, shifted(): return lax.ppermute(x, axis, pairs)  13.4 us
    unnamed x5, local copies, waits for them, and re-layouts  5.37 us
    ppermute x8, waiting for transfers between devices, shifted(): return lax.ppermute(x, axis, pairs)  4.22 us
    dot_general x2, matrix products, apply_operator(): lax.dot_general(left_env[0], stacked, (((0, 2), (0, 1)), ((), ())), prefe...  4.22 us
  transfers between devices with their start and end apart: 8, of which 2 were waited for; matrix products, arithmetic and copies ran while one was open for 9% of the time, Pallas kernels for 0%

commit v1 on v0

v1 whole, which is shorter than its diff:
```python
import functools

import jax
import jax.numpy as jnp
from jax import lax
from jax.experimental import pallas as pl
from jax.experimental.pallas import tpu as pltpu
from jax.sharding import PartitionSpec as P

QD = 8
SCALE = 1024.0
NT = (((1,), (1,)), ((), ()))
VM = pl.BlockSpec(memory_space=pltpu.VMEM)
SM = pl.BlockSpec(memory_space=pltpu.SMEM)
PARAMS = pltpu.CompilerParams(vmem_limit_bytes=24 * 1024 * 1024)


def swap(x, axis, pairs):
    return lax.ppermute(x, axis, [(a, b) for a, b in pairs] + [(b, a) for a, b in pairs])


def swap_pairs(size):
    rows = size // QD
    near = [(s, s + 1) for s in range(0, size, 2)]
    far = [(s, s + 1) for s in range(1, size - 1, 2) if s % QD != QD - 1]
    row_even = [(s, s + QD) for r in range(0, rows - 1, 2) for s in range(r * QD, r * QD + QD)]
    row_odd = [(s, s + QD) for r in range(1, rows - 1, 2) for s in range(r * QD, r * QD + QD)]
    return near, far, [p for p in (row_even, row_odd) if p]


def live(dims_ref, shape):
    row_ok = lax.broadcasted_iota(jnp.int32, shape, 0) < dims_ref[0, 0]
    col_ok = lax.broadcasted_iota(jnp.int32, shape, 1) < dims_ref[0, 1]
    return row_ok & col_ok


def total(x):
    return jnp.sum(jnp.sum(x, axis=0, keepdims=True), axis=1, keepdims=True)


def terms(src, left_ref, right_ref, offset, count):
    size = src.shape[0]
    right = right_ref[pl.ds(offset, count)].reshape(count * size, size)
    partial_t = lax.dot_general(right, src, NT, preferred_element_type=jnp.float32).astype(jnp.bfloat16)
    image = None
    for k in range(count):
        piece = lax.dot_general(
            left_ref[offset + k], partial_t[k * size : (k + 1) * size], NT, preferred_element_type=jnp.float32
        )
        image = piece if image is None else image + piece
    return image


def start_kernel(dims_ref, wave_ref, u_ref, norm_ref):
    wave = wave_ref[0]
    held = jnp.where(live(dims_ref, wave.shape), wave, 0.0)
    u_ref[...] = (held * SCALE).astype(jnp.bfloat16)
    norm_ref[...] = jnp.broadcast_to(total(held * held), norm_ref.shape)


def near_kernel(width, offs_ref, self_ref, near_ref, far_ref, left_ref, right_ref, out_ref):
    left_ref, right_ref = left_ref.at[0], right_ref.at[0]
    out_ref[0] = terms(self_ref[...], left_ref, right_ref, 0, 2)
    out_ref[1] = terms(near_ref[...], left_ref, right_ref, offs_ref[0], width)
    out_ref[2] = terms(far_ref[...], left_ref, right_ref, offs_ref[1], width)


def near_sum_kernel(width, offs_ref, self_ref, near_ref, far_ref, left_ref, right_ref, out_ref):
    left_ref, right_ref = left_ref.at[0], right_ref.at[0]
    out_ref[...] = (
        terms(self_ref[...], left_ref, right_ref, 0, 2)
        + terms(near_ref[...], left_ref, right_ref, offs_ref[0], width)
        + terms(far_ref[...], left_ref, right_ref, offs_ref[1], width)
    )


def first_kernel(width, rows, offs_ref, dims_ref, u_ref, norm_ref, part_ref, left_ref, right_ref, *refs):
    row_refs, (row_out_ref, image_ref, w_ref, stats_ref) = refs[:rows], refs[rows:]
    left_ref, right_ref = left_ref.at[0], right_ref.at[0]
    image = part_ref[0] + part_ref[1] + part_ref[2]
    for r in range(rows):
        piece = terms(row_refs[r][...], left_ref, right_ref, offs_ref[2 + r], width)
        row_out_ref[r] = piece
        image = image + piece
    image = jnp.where(live(dims_ref, image.shape), image, 0.0)
    image_ref[...] = image
    u = u_ref[...].astype(jnp.float32)
    square = total(u * u)
    cross = total(u * image)
    rho = jnp.where(square > 0.0, cross / square, 0.0)
    w = image - rho * u
    w_ref[...] = w.astype(jnp.bfloat16)
    lines = lax.broadcasted_iota(jnp.int32, (8, 128), 0)
    stats = jnp.where(lines == 0, norm_ref[...], 0.0)
    for line, value in ((1, square), (2, cross), (3, total(w * w)), (4, rho)):
        stats = jnp.where(lines == line, value, stats)
    stats_ref[...] = jnp.broadcast_to(stats[None], stats_ref.shape)


def second_kernel(width, rows, cells, offs_ref, dims_ref, stats_ref, hw_ref, part_ref, row_part_ref, image_ref,
                  left_ref, right_ref, *refs):
    row_refs, (first_ref, second_ref) = refs[:rows], refs[rows:]
    left_ref, right_ref = left_ref.at[0], right_ref.at[0]
    stats = stats_ref[...]
    sums = jnp.sum(stats, axis=0)
    start, square, cross, inner = (sums[i : i + 1, 0:1] for i in range(4))
    rho = cross / square
    gap = stats[:, 4:5, 0:1] - rho[None]
    residual = inner + jnp.sum(stats[:, 1:2, 0:1] * gap * gap, axis=0)
    scale = lax.rsqrt(start / cells + 1e-06) * (1.0 / SCALE)
    second_scale = scale * lax.rsqrt(scale * scale * (residual / cells) + 1e-06)
    image = hw_ref[...]
    for n in range(3):
        image = image + (stats_ref[offs_ref[8 + n], 4:5, 0:1] - rho) * part_ref[n]
    for r in range(rows):
        image = image + (stats_ref[offs_ref[11 + r], 4:5, 0:1] - rho) * row_part_ref[r]
        image = image + terms(row_refs[r][...], left_ref, right_ref, offs_ref[2 + r], width)
    first_ref[0] = image_ref[...] * scale
    second_ref[0] = jnp.where(live(dims_ref, image.shape), image, 0.0) * second_scale


def body(wavefunction, sector_dims, left_env, right_env):
    size = lax.axis_size("sector")
    block = wavefunction.shape[1]
    square = (block, block)
    width = (right_env.shape[1] - 2) // 4
    near, far, row_pairs = swap_pairs(size)
    rows = len(row_pairs)
    cells = float(size * block * block)

    me = lax.axis_index("sector")
    odd = (me % QD) % 2
    row_odd = (me // QD) % 2
    low, high, down, up = 2, 2 + width, 2 + 2 * width, 2 + 3 * width
    near_off = jnp.where(odd == 1, low, high)
    far_off = jnp.where(odd == 1, high, low)
    even_off = jnp.where(row_odd == 1, down, up)
    odd_off = jnp.where(row_odd == 1, up, down)
    partners = [me, jnp.where(odd == 1, me - 1, me + 1), jnp.where(odd == 1, me + 1, me - 1),
                jnp.where(row_odd == 1, me - QD, me + QD), jnp.where(row_odd == 1, me + QD, me - QD)]
    partners = [jnp.clip(p, 0, size - 1) for p in partners]
    zero = jnp.int32(0)
    offs = jnp.stack([near_off, far_off, even_off, odd_off, zero, zero, zero, zero] + partners + [zero] * 3)
    offs = offs.astype(jnp.int32)

    f32 = jnp.float32
    sds = jax.ShapeDtypeStruct
    u, norm = pl.pallas_call(
        start_kernel, out_shape=(sds(square, jnp.bfloat16), sds((8, 128), f32)),
        in_specs=[SM, VM], out_specs=(VM, VM), compiler_params=PARAMS,
    )(sector_dims, wavefunction)

    row_u = [swap(u, "sector", p) for p in row_pairs]
    near_u = swap(u, "sector", near)
    far_u = swap(u, "sector", far)
    part = pl.pallas_call(
        functools.partial(near_kernel, width), out_shape=sds((3,) + square, f32),
        in_specs=[SM] + [VM] * 5, out_specs=VM, compiler_params=PARAMS,
    )(offs, u, near_u, far_u, left_env, right_env)
    row_part, image, w, stats = pl.pallas_call(
        functools.partial(first_kernel, width, rows),
        out_shape=(sds((rows,) + square, f32), sds(square, f32), sds(square, jnp.bfloat16), sds((size, 8, 128), f32)),
        in_specs=[SM, SM] + [VM] * (5 + rows), out_specs=(VM,) * 4, compiler_params=PARAMS,
    )(offs, sector_dims, u, norm, part, left_env, right_env, *row_u)

    row_w = [swap(w, "sector", p) for p in row_pairs]
    near_w = swap(w, "sector", near)
    far_w = swap(w, "sector", far)
    stats = lax.all_to_all(stats, "sector", 0, 0, tiled=True)
    hw = pl.pallas_call(
        functools.partial(near_sum_kernel, width), out_shape=sds(square, f32),
        in_specs=[SM] + [VM] * 5, out_specs=VM, compiler_params=PARAMS,
    )(offs, w, near_w, far_w, left_env, right_env)
    return pl.pallas_call(
        functools.partial(second_kernel, width, rows, cells),
        out_shape=(sds((1,) + square, f32),) * 2,
        in_specs=[SM, SM] + [VM] * (7 + rows), out_specs=(VM, VM), compiler_params=PARAMS,
    )(offs, sector_dims, stats, hw, part, row_part, image, left_env, right_env, *row_w)


def solution(mesh):
    placed = (
        P(("groups", "sector"), None, None),
        P(("groups", "sector"), None),
        P(("groups", "sector"), None, None, None),
        P(("groups", "sector"), None, None, None),
    )
    return jax.shard_map(
        body,
        mesh=mesh,
        in_specs=placed,
        out_specs=(P(("groups", "sector"), None, None), P(("groups", "sector"), None, None)),
        check_vma=False,
    )
```

time: 153 us -> 52 us (0.34)
  blocking collectives: 98.6 us -> 0 us
  matrix products: 19.1 us -> 0 us
  local copies, waits for them, and re-layouts: 6.78 us -> 19.9 us
  Pallas kernels: 0 us -> 10.1 us
  other arithmetic: 7.04 us -> 0 us
  starting transfers between devices: 13.4 us -> 18.8 us
  between operations: 3.56 us -> 0.78 us
  waiting for transfers between devices: 4.22 us -> 1.79 us
    psum x3 -> x0, blocking collectives: 98.6 us -> none  [the longest x1 35.5 us: body(): start_norm = lax.psum(local_norm, 'sector')]
    dot_general x12 -> x0, matrix products: 19.1 us -> none  [the longest x10 14.8 us: apply_operator(): jnp.einsum('ab,kcb->kac', sources[number][0], right_env[0, bounds[number]...]
    unnamed x5 -> x44, local copies, waits for them, and re-layouts: 5.37 us -> 19.8 us
    pallas_call x0 -> x5, Pallas kernels: none -> 10.1 us  [the longest x1 2.53 us: body(): pl.pallas_call(functools.partial(first_kernel, width, rows), out_shape=(s...]
    all_to_all x0 -> x1, starting transfers between devices: none -> 4.22 us  [body(): stats = lax.all_to_all(stats, 'sector', 0, 0, tiled=True)]
    ppermute x8 -> x6, waiting for transfers between devices: 4.22 us -> 0.02 us  [swap(): lax.ppermute(x, axis, [(a, b) for a, b in pairs] + [(b, a) for a, b in pa...]
    reduce_sum x2 -> x0, other arithmetic: 3.48 us -> none  [the longest x1 1.78 us: body(): residual_norm = lax.psum(jnp.sum(residual_field * residual_field), 'sector')]
    convert_element_type x2 -> x0, other arithmetic: 2.23 us -> none  [the longest x1 1.17 us: body(): (residual_field * lax.rsqrt(residual_norm / cell_count + 1e-06)).astype(j...]
  transfers between devices with their start and end apart: 8 -> 7, of which waited for: 2 -> 1; matrix products, arithmetic and copies ran while one was open for 9% -> 0% of each run, Pallas kernels for 0% -> 8%
where the time goes in v1:
time: 52 us; the launch traced here: 51.3 us
  local copies, waits for them, and re-layouts  19.9 us (38%)
  starting transfers between devices  18.8 us (36%)
  Pallas kernels  10.1 us (19%)
  waiting for transfers between devices  1.79 us (3%)
  between operations  0.78 us (2%)
    unnamed x44, local copies, waits for them, and re-layouts  19.8 us
    ppermute x6, starting transfers between devices, swap(): lax.ppermute(x, axis, [(a, b) for a, b in pairs] + [(b, a) for a, b in pa...  14.6 us
    all_to_all x1, starting transfers between devices, body(): stats = lax.all_to_all(stats, 'sector', 0, 0, tiled=True)  4.22 us
    pallas_call x1, Pallas kernels, body(): pl.pallas_call(functools.partial(first_kernel, width, rows), out_shape=(s...  2.53 us
    pallas_call x1, Pallas kernels, body(): pl.pallas_call(functools.partial(second_kernel, width, rows, cells), out_...  2.52 us
    pallas_call x1, Pallas kernels, body(): pl.pallas_call(functools.partial(near_sum_kernel, width), out_shape=sds(s...  2.42 us
    pallas_call x1, Pallas kernels, body(): pl.pallas_call(functools.partial(near_kernel, width), out_shape=sds((3,)...  1.92 us
    all_to_all x1, waiting for transfers between devices, body(): stats = lax.all_to_all(stats, 'sector', 0, 0, tiled=True)  1.77 us
  transfers between devices with their start and end apart: 7, of which 1 were waited for; matrix products, arithmetic and copies ran while one was open for 0% of the time, Pallas kernels for 8%

profile of v1, /device:TPU:0, one launch (start us, length us, event | category | flops | bytes accessed | tf_op | source)
XLA Modules:
  0.0 51.3 jit_solution(962244078745368737)
XLA Ops:
  0.6 0.9 %copy-done.14 = f32[1,256,256]{2,1,0:T(8,128)S(1)} copy-done((f32[1,256,256]{2,1,0:T(8,128)S(1)}, f32[1,256,256]{2,1,0:T(8,128)}, u32[]{:S(2)}) %copy-start.14) | copy-done | bytes 262168
  3.6 4.4 %collective-permute-start = (bf16[256,256]{1,0:T(8,128)(2,1)S(1)}, bf16[256,256]{1,0:T(8,128)(2,1)S(1)}, u32[]{:S(2)}, u32[]{:S(2)}) collective-permute-start(bf16[256,256]{1,0:T(8,128)(2,1)S(1)} %get-tuple-element.8.self_ref.u_ref), channel_id=1, source_target_pairs={{0,1},{2,3},{4,5},{6,7},{8,9},{10,11},{12,13},{14,15},{1,0},{3,2},... | collective-permute-start | bytes 393224 | tf_op jit(solution)/shard_map/ppermute | solution.py:19
  8.0 2.6 %collective-permute-start.2 = (bf16[256,256]{1,0:T(8,128)(2,1)S(1)}, bf16[256,256]{1,0:T(8,128)(2,1)}, u32[]{:S(2)}, u32[]{:S(2)}) collective-permute-start(bf16[256,256]{1,0:T(8,128)(2,1)S(1)} %get-tuple-element.8.self_ref.u_ref), channel_id=1, source_target_pairs={{0,8},{1,9},{2,10},{3,11},{4,12},{5,13},{6,14},{7,15},{8,0},{9,1},... | collective-permute-start | bytes 393224 | tf_op jit(solution)/shard_map/ppermute | solution.py:19
  12.0 2.0 %copy-done = bf16[1,26,256,256]{3,2,1,0:T(8,128)(2,1)S(1)} copy-done((bf16[1,26,256,256]{3,2,1,0:T(8,128)(2,1)S(1)}, bf16[1,26,256,256]{3,2,1,0:T(8,128)(2,1)}, u32[]{:S(2)}) %copy-start) | copy-done | bytes 3407896
  13.9 2.0 %copy-done.2 = bf16[1,26,256,256]{3,2,1,0:T(8,128)(2,1)S(1)} copy-done((bf16[1,26,256,256]{3,2,1,0:T(8,128)(2,1)S(1)}, bf16[1,26,256,256]{3,2,1,0:T(8,128)(2,1)}, u32[]{:S(2)}) %copy-start.2) | copy-done | bytes 3407896
  15.9 0.9 %copy-done.16 = bf16[256,256]{1,0:T(8,128)(2,1)S(1)} copy-done((bf16[256,256]{1,0:T(8,128)(2,1)S(1)}, bf16[256,256]{1,0:T(8,128)(2,1)}, u32[]{:S(2)}) %copy-start.16) | copy-done | bytes 131096
  16.8 0.9 %copy-done.18 = bf16[256,256]{1,0:T(8,128)(2,1)S(1)} copy-done((bf16[256,256]{1,0:T(8,128)(2,1)S(1)}, bf16[256,256]{1,0:T(8,128)(2,1)}, u32[]{:S(2)}) %copy-start.18) | copy-done | bytes 131096
  17.7 1.9 %shard_map.60.part_ref = f32[3,256,256]{2,1,0:T(8,128)S(1)} custom-call(s32[16]{0:T(128)S(1)} %stack.39.offs_ref, bf16[256,256]{1,0:T(8,128)(2,1)S(1)} %get-tuple-element.8.self_ref.u_ref, bf16[256,256]{1,0:T(8,128)(2,1)S(1)} %copy-done.18, bf16[256,256]{1,0:T(8,128)(2,1)S(1)} %copy-done.16, bf16[1,26,256,256]{3,2,1,0:T(8,128)(2,1)S(1)} %copy-done, ...), custom_call_target="tpu_custom_call" | custom-call | tf_op jit(solution)/shard_map/pallas_call | solution.py:156
  19.7 1.1 %copy-done.3 = bf16[1,26,256,256]{3,2,1,0:T(8,128)(2,1)S(1)} copy-done((bf16[1,26,256,256]{3,2,1,0:T(8,128)(2,1)S(1)}, bf16[1,26,256,256]{3,2,1,0:T(8,128)(2,1)}, u32[]{:S(2)}) %copy-start.3) | copy-done | bytes 3407896
  20.8 2.5 %shard_map.61 = (f32[1,256,256]{2,1,0:T(8,128)S(1)}, f32[256,256]{1,0:T(8,128)S(1)}, bf16[256,256]{1,0:T(8,128)(2,1)}, f32[16,8,128]{2,1,0:T(8,128)S(1)}) custom-call(s32[16]{0:T(128)S(1)} %stack.39.offs_ref, s32[1,2]{1,0:T(1,128)S(1)} %copy-done.21, bf16[256,256]{1,0:T(8,128)(2,1)S(1)} %get-tuple-element.8.self_ref.u_ref, ...), custom_call_target="tpu_custom_call" | custom-call | tf_op jit(solution)/shard_map/pallas_call | solution.py:160
  24.1 0.7 %copy-done.12 = f32[256,256]{1,0:T(8,128)} copy-done((f32[256,256]{1,0:T(8,128)}, f32[256,256]{1,0:T(8,128)S(1)}, u32[]{:S(2)}) %copy-start.12) | copy-done | bytes 262168
  24.8 1.3 %collective-permute-start.4 = (bf16[256,256]{1,0:T(8,128)(2,1)}, bf16[256,256]{1,0:T(8,128)(2,1)}, u32[]{:S(2)}, u32[]{:S(2)}) collective-permute-start(bf16[256,256]{1,0:T(8,128)(2,1)} %get-tuple-element.11.self_ref), channel_id=1, source_target_pairs={{1,2},{3,4},{5,6},{9,10},{11,12},{13,14},{2,1},{4,3},{6,5},{10,9},... | collective-permute-start | bytes 393224 | tf_op jit(solution)/shard_map/ppermute | solution.py:19
  26.1 3.7 %collective-permute-start.3 = (bf16[256,256]{1,0:T(8,128)(2,1)}, bf16[256,256]{1,0:T(8,128)(2,1)}, u32[]{:S(2)}, u32[]{:S(2)}) collective-permute-start(bf16[256,256]{1,0:T(8,128)(2,1)} %get-tuple-element.11.self_ref), channel_id=1, source_target_pairs={{0,1},{2,3},{4,5},{6,7},{8,9},{10,11},{12,13},{14,15},{1,0},{3,2},... | collective-permute-start | bytes 393224 | tf_op jit(solution)/shard_map/ppermute | solution.py:19
  29.7 2.0 %collective-permute-start.5 = (bf16[256,256]{1,0:T(8,128)(2,1)}, bf16[256,256]{1,0:T(8,128)(2,1)}, u32[]{:S(2)}, u32[]{:S(2)}) collective-permute-start(bf16[256,256]{1,0:T(8,128)(2,1)} %get-tuple-element.11.self_ref), channel_id=1, source_target_pairs={{0,8},{1,9},{2,10},{3,11},{4,12},{5,13},{6,14},{7,15},{8,0},{9,1},... | collective-permute-start | bytes 393224 | tf_op jit(solution)/shard_map/ppermute | solution.py:19
  31.7 4.2 %all-to-all-start = ((f32[16,8,128]{2,1,0:T(8,128)}), f32[16,8,128]{2,1,0:T(8,128)S(1)}, u32[]{:S(2)}, u32[]{:S(2)}) async-start(f32[16,8,128]{2,1,0:T(8,128)} %copy-done.19), calls=%async_computation | async-start | bytes 131072 | tf_op jit(solution)/shard_map/all_to_all | solution.py:169
  36.0 2.0 %copy-done.4 = bf16[1,26,256,256]{3,2,1,0:T(8,128)(2,1)S(1)} copy-done((bf16[1,26,256,256]{3,2,1,0:T(8,128)(2,1)S(1)}, bf16[1,26,256,256]{3,2,1,0:T(8,128)(2,1)}, u32[]{:S(2)}) %copy-start.4) | copy-done | bytes 3407896
  38.0 2.4 %shard_map.62.hw_ref = f32[256,256]{1,0:T(8,128)S(1)} custom-call(s32[16]{0:T(128)S(1)} %stack.39.offs_ref, bf16[256,256]{1,0:T(8,128)(2,1)} %get-tuple-element.11.self_ref, bf16[256,256]{1,0:T(8,128)(2,1)} %collective-permute-done.3.near_ref, bf16[256,256]{1,0:T(8,128)(2,1)} %collective-permute-done.4.far_ref, bf16[1,26,256,256]{3,2,1,0:T(8,128)(2,1)S(1)} %copy-done.1, ...), custom_call_target="tpu_custom_call" | custom-call | tf_op jit(solution)/shard_map/pallas_call | solution.py:170
  41.1 1.8 %all-to-all-done.stats_ref = f32[16,8,128]{2,1,0:T(8,128)S(1)} async-done(((f32[16,8,128]{2,1,0:T(8,128)}), f32[16,8,128]{2,1,0:T(8,128)S(1)}, u32[]{:S(2)}, u32[]{:S(2)}) %all-to-all-start) | async-done | bytes 65568 | tf_op jit(solution)/shard_map/all_to_all | solution.py:169
  42.9 2.0 %copy-done.5 = bf16[1,26,256,256]{3,2,1,0:T(8,128)(2,1)S(1)} copy-done((bf16[1,26,256,256]{3,2,1,0:T(8,128)(2,1)S(1)}, bf16[1,26,256,256]{3,2,1,0:T(8,128)(2,1)}, u32[]{:S(2)}) %copy-start.5) | copy-done | bytes 3407896
  44.8 1.1 %copy-done.7 = f32[3,256,256]{2,1,0:T(8,128)S(1)} copy-done((f32[3,256,256]{2,1,0:T(8,128)S(1)}, f32[3,256,256]{2,1,0:T(8,128)}, u32[]{:S(2)}) %copy-start.7) | copy-done | bytes 786456
  46.0 0.9 %copy-done.9 = f32[256,256]{1,0:T(8,128)S(1)} copy-done((f32[256,256]{1,0:T(8,128)S(1)}, f32[256,256]{1,0:T(8,128)}, u32[]{:S(2)}) %copy-start.9) | copy-done | bytes 262168
  46.9 0.9 %copy-done.11 = f32[1,256,256]{2,1,0:T(8,128)S(1)} copy-done((f32[1,256,256]{2,1,0:T(8,128)S(1)}, f32[1,256,256]{2,1,0:T(8,128)}, u32[]{:S(2)}) %copy-start.11) | copy-done | bytes 262168
  47.9 0.9 %copy-done.13 = f32[256,256]{1,0:T(8,128)S(1)} copy-done((f32[256,256]{1,0:T(8,128)S(1)}, f32[256,256]{1,0:T(8,128)}, u32[]{:S(2)}) %copy-start.13) | copy-done | bytes 262168
  48.8 2.5 %shard_map.63 = (f32[1,256,256]{2,1,0:T(8,128)}, f32[1,256,256]{2,1,0:T(8,128)}) custom-call(s32[16]{0:T(128)S(1)} %stack.39.offs_ref, s32[1,2]{1,0:T(1,128)S(1)} %copy-done.21, f32[16,8,128]{2,1,0:T(8,128)S(1)} %all-to-all-done.stats_ref, f32[256,256]{1,0:T(8,128)S(1)} %copy-done.9, f32[3,256,256]{2,1,0:T(8,128)S(1)} %copy-done.7, ...), custom_call_target="tpu_custom_call" | custom-call | tf_op jit(solution)/shard_map/pallas_call | solution.py:174
  (42 shorter events, 4.9 us)
Async XLA Ops:
  0.6 1.0 %copy-start.14 = (f32[1,256,256]{2,1,0:T(8,128)S(1)}, f32[1,256,256]{2,1,0:T(8,128)}, u32[]{:S(2)}) copy-start(f32[1,256,256]{2,1,0:T(8,128)} %wave_ref.1) | copy-start | bytes 786436
  2.9 7.7 %collective-permute-start.1 = (bf16[256,256]{1,0:T(8,128)(2,1)S(1)}, bf16[256,256]{1,0:T(8,128)(2,1)S(1)}, u32[]{:S(2)}, u32[]{:S(2)}) collective-permute-start(bf16[256,256]{1,0:T(8,128)(2,1)S(1)} %get-tuple-element.8.self_ref.u_ref), channel_id=1, source_target_pairs={{1,2},{3,4},{5,6},{9,10},{11,12},{13,14},{2,1},{4,3},{6,5},{10,9},... | collective-permute-start | bytes 393224 | tf_op jit(solution)/shard_map/ppermute | solution.py:19
  3.6 7.7 %collective-permute-start = (bf16[256,256]{1,0:T(8,128)(2,1)S(1)}, bf16[256,256]{1,0:T(8,128)(2,1)S(1)}, u32[]{:S(2)}, u32[]{:S(2)}) collective-permute-start(bf16[256,256]{1,0:T(8,128)(2,1)S(1)} %get-tuple-element.8.self_ref.u_ref), channel_id=1, source_target_pairs={{0,1},{2,3},{4,5},{6,7},{8,9},{10,11},{12,13},{14,15},{1,0},{3,2},... | collective-permute-start | bytes 393224 | tf_op jit(solution)/shard_map/ppermute | solution.py:19
  8.0 11.7 %collective-permute-start.2 = (bf16[256,256]{1,0:T(8,128)(2,1)S(1)}, bf16[256,256]{1,0:T(8,128)(2,1)}, u32[]{:S(2)}, u32[]{:S(2)}) collective-permute-start(bf16[256,256]{1,0:T(8,128)(2,1)S(1)} %get-tuple-element.8.self_ref.u_ref), channel_id=1, source_target_pairs={{0,8},{1,9},{2,10},{3,11},{4,12},{5,13},{6,14},{7,15},{8,0},{9,1},... | collective-permute-start | bytes 393224 | tf_op jit(solution)/shard_map/ppermute | solution.py:19
  10.6 9.1 %copy-start.21 = (s32[1,2]{1,0:T(1,128)S(1)}, s32[1,2]{1,0:T(1,128)}, u32[]{:S(2)}) copy-start(s32[1,2]{1,0:T(1,128)} %dims_ref.5) | copy-start | bytes 28
  12.0 2.0 %copy-start = (bf16[1,26,256,256]{3,2,1,0:T(8,128)(2,1)S(1)}, bf16[1,26,256,256]{3,2,1,0:T(8,128)(2,1)}, u32[]{:S(2)}) copy-start(bf16[1,26,256,256]{3,2,1,0:T(8,128)(2,1)} %left_ref.7) | copy-start | bytes 10223620
  13.9 2.0 %copy-start.2 = (bf16[1,26,256,256]{3,2,1,0:T(8,128)(2,1)S(1)}, bf16[1,26,256,256]{3,2,1,0:T(8,128)(2,1)}, u32[]{:S(2)}) copy-start(bf16[1,26,256,256]{3,2,1,0:T(8,128)(2,1)} %right_ref.7) | copy-start | bytes 10223620
  15.9 0.9 %copy-start.16 = (bf16[256,256]{1,0:T(8,128)(2,1)S(1)}, bf16[256,256]{1,0:T(8,128)(2,1)}, u32[]{:S(2)}) copy-start(bf16[256,256]{1,0:T(8,128)(2,1)} %copy-done.15) | copy-start | bytes 393220
  16.8 0.9 %copy-start.18 = (bf16[256,256]{1,0:T(8,128)(2,1)S(1)}, bf16[256,256]{1,0:T(8,128)(2,1)}, u32[]{:S(2)}) copy-start(bf16[256,256]{1,0:T(8,128)(2,1)} %copy-done.17) | copy-start | bytes 393220
  17.7 2.0 %copy-start.1 = (bf16[1,26,256,256]{3,2,1,0:T(8,128)(2,1)S(1)}, bf16[1,26,256,256]{3,2,1,0:T(8,128)(2,1)}, u32[]{:S(2)}) copy-start(bf16[1,26,256,256]{3,2,1,0:T(8,128)(2,1)} %left_ref.7) | copy-start | bytes 10223620
  17.7 3.1 %copy-start.3 = (bf16[1,26,256,256]{3,2,1,0:T(8,128)(2,1)S(1)}, bf16[1,26,256,256]{3,2,1,0:T(8,128)(2,1)}, u32[]{:S(2)}) copy-start(bf16[1,26,256,256]{3,2,1,0:T(8,128)(2,1)} %right_ref.7) | copy-start | bytes 10223620
  19.6 3.7 %copy-start.6 = (f32[3,256,256]{2,1,0:T(8,128)}, f32[3,256,256]{2,1,0:T(8,128)S(1)}, u32[]{:S(2)}) copy-start(f32[3,256,256]{2,1,0:T(8,128)S(1)} %shard_map.60.part_ref) | copy-start | bytes 2359300
  24.1 0.7 %copy-start.12 = (f32[256,256]{1,0:T(8,128)}, f32[256,256]{1,0:T(8,128)S(1)}, u32[]{:S(2)}) copy-start(f32[256,256]{1,0:T(8,128)S(1)} %get-tuple-element.13.image_ref) | copy-start | bytes 786436
  24.8 7.0 %copy-start.19 = (f32[16,8,128]{2,1,0:T(8,128)}, f32[16,8,128]{2,1,0:T(8,128)S(1)}, u32[]{:S(2)}) copy-start(f32[16,8,128]{2,1,0:T(8,128)S(1)} %get-tuple-element.10) | copy-start | bytes 196612
  24.8 11.2 %collective-permute-start.4 = (bf16[256,256]{1,0:T(8,128)(2,1)}, bf16[256,256]{1,0:T(8,128)(2,1)}, u32[]{:S(2)}, u32[]{:S(2)}) collective-permute-start(bf16[256,256]{1,0:T(8,128)(2,1)} %get-tuple-element.11.self_ref), channel_id=1, source_target_pairs={{1,2},{3,4},{5,6},{9,10},{11,12},{13,14},{2,1},{4,3},{6,5},{10,9},... | collective-permute-start | bytes 393224 | tf_op jit(solution)/shard_map/ppermute | solution.py:19
  26.1 9.9 %collective-permute-start.3 = (bf16[256,256]{1,0:T(8,128)(2,1)}, bf16[256,256]{1,0:T(8,128)(2,1)}, u32[]{:S(2)}, u32[]{:S(2)}) collective-permute-start(bf16[256,256]{1,0:T(8,128)(2,1)} %get-tuple-element.11.self_ref), channel_id=1, source_target_pairs={{0,1},{2,3},{4,5},{6,7},{8,9},{10,11},{12,13},{14,15},{1,0},{3,2},... | collective-permute-start | bytes 393224 | tf_op jit(solution)/shard_map/ppermute | solution.py:19
  29.7 13.1 %collective-permute-start.5 = (bf16[256,256]{1,0:T(8,128)(2,1)}, bf16[256,256]{1,0:T(8,128)(2,1)}, u32[]{:S(2)}, u32[]{:S(2)}) collective-permute-start(bf16[256,256]{1,0:T(8,128)(2,1)} %get-tuple-element.11.self_ref), channel_id=1, source_target_pairs={{0,8},{1,9},{2,10},{3,11},{4,12},{5,13},{6,14},{7,15},{8,0},{9,1},... | collective-permute-start | bytes 393224 | tf_op jit(solution)/shard_map/ppermute | solution.py:19
  31.7 11.1 %all-to-all-start = ((f32[16,8,128]{2,1,0:T(8,128)}), f32[16,8,128]{2,1,0:T(8,128)S(1)}, u32[]{:S(2)}, u32[]{:S(2)}) async-start(f32[16,8,128]{2,1,0:T(8,128)} %copy-done.19), calls=%async_computation | async-start | bytes 131072 | tf_op jit(solution)/shard_map/all_to_all | solution.py:169
  36.0 2.0 %copy-start.4 = (bf16[1,26,256,256]{3,2,1,0:T(8,128)(2,1)S(1)}, bf16[1,26,256,256]{3,2,1,0:T(8,128)(2,1)}, u32[]{:S(2)}) copy-start(bf16[1,26,256,256]{3,2,1,0:T(8,128)(2,1)} %right_ref.7) | copy-start | bytes 10223620
  42.9 2.0 %copy-start.5 = (bf16[1,26,256,256]{3,2,1,0:T(8,128)(2,1)S(1)}, bf16[1,26,256,256]{3,2,1,0:T(8,128)(2,1)}, u32[]{:S(2)}) copy-start(bf16[1,26,256,256]{3,2,1,0:T(8,128)(2,1)} %right_ref.7) | copy-start | bytes 10223620
  44.8 1.1 %copy-start.7 = (f32[3,256,256]{2,1,0:T(8,128)S(1)}, f32[3,256,256]{2,1,0:T(8,128)}, u32[]{:S(2)}) copy-start(f32[3,256,256]{2,1,0:T(8,128)} %copy-done.6) | copy-start | bytes 2359300
  46.0 0.9 %copy-start.9 = (f32[256,256]{1,0:T(8,128)S(1)}, f32[256,256]{1,0:T(8,128)}, u32[]{:S(2)}) copy-start(f32[256,256]{1,0:T(8,128)} %copy-done.8) | copy-start | bytes 786436
  46.9 0.9 %copy-start.11 = (f32[1,256,256]{2,1,0:T(8,128)S(1)}, f32[1,256,256]{2,1,0:T(8,128)}, u32[]{:S(2)}) copy-start(f32[1,256,256]{2,1,0:T(8,128)} %copy-done.10) | copy-start | bytes 786436
  47.9 0.9 %copy-start.13 = (f32[256,256]{1,0:T(8,128)S(1)}, f32[256,256]{1,0:T(8,128)}, u32[]{:S(2)}) copy-start(f32[256,256]{1,0:T(8,128)} %copy-done.12) | copy-start | bytes 786436
  (5 other events, 3.4 us)

commit v2 on v1

v2 whole, which is shorter than its diff:
```python
import functools

import jax
import jax.numpy as jnp
from jax import lax
from jax.experimental import pallas as pl
from jax.experimental.pallas import tpu as pltpu
from jax.sharding import PartitionSpec as P

QD = 8
SCALE = 1024.0
NT = (((1,), (1,)), ((), ()))
VM = pl.BlockSpec(memory_space=pltpu.VMEM)
HB = pl.BlockSpec(memory_space=pltpu.HBM)
PARAMS = pltpu.CompilerParams(vmem_limit_bytes=16 * 1024 * 1024)


def vmem(x):
    return pltpu.with_memory_space_constraint(x, pltpu.VMEM)


def hbm(x):
    return pltpu.with_memory_space_constraint(x, pltpu.HBM)


def swap(x, axis, pairs):
    return lax.ppermute(x, axis, [(a, b) for a, b in pairs] + [(b, a) for a, b in pairs])


def swap_pairs(size):
    rows = size // QD
    near = [(s, s + 1) for s in range(0, size, 2)]
    far = [(s, s + 1) for s in range(1, size - 1, 2) if s % QD != QD - 1]
    row_even = [(s, s + QD) for r in range(0, rows - 1, 2) for s in range(r * QD, r * QD + QD)]
    row_odd = [(s, s + QD) for r in range(1, rows - 1, 2) for s in range(r * QD, r * QD + QD)]
    return near, far, [p for p in (row_even, row_odd) if p]


def place(size, width):
    me = lax.axis_index("sector")
    odd = lax.rem(me, 2) == 1
    row_odd = lax.rem(lax.div(me, QD), 2) == 1
    low, high, down, up = 2, 2 + width, 2 + 2 * width, 2 + 3 * width
    offsets = [jnp.where(odd, low, high), jnp.where(odd, high, low),
               jnp.where(row_odd, down, up), jnp.where(row_odd, up, down)]
    steps = [jnp.where(odd, -1, 1), jnp.where(odd, 1, -1), jnp.where(row_odd, -QD, QD), jnp.where(row_odd, QD, -QD)]
    partners = [me] + [jnp.clip(me + step, 0, size - 1) for step in steps]
    return offsets, partners


def live(facts, shape):
    row_ok = lax.broadcasted_iota(jnp.int32, shape, 0).astype(jnp.float32) < facts[1:2, 0:1]
    col_ok = lax.broadcasted_iota(jnp.int32, shape, 1).astype(jnp.float32) < facts[2:3, 0:1]
    return row_ok & col_ok


def total(x):
    return jnp.sum(jnp.sum(x, axis=0, keepdims=True), axis=1, keepdims=True)


def terms(src, left_ref, right_ref, offset, count):
    size = src.shape[0]
    right = right_ref[pl.ds(offset, count)].reshape(count * size, size)
    partial_t = lax.dot_general(right, src, NT, preferred_element_type=jnp.float32).astype(jnp.bfloat16)
    image = None
    for k in range(count):
        piece = lax.dot_general(
            left_ref[offset + k], partial_t[k * size : (k + 1) * size], NT, preferred_element_type=jnp.float32
        )
        image = piece if image is None else image + piece
    return image


def start_kernel(wave_hbm, dims_hbm, u_ref, facts_ref, wave_ref, dims_ref, sems):
    wave_copy = pltpu.make_async_copy(wave_hbm.at[0], wave_ref, sems.at[0])
    dims_copy = pltpu.make_async_copy(dims_hbm, dims_ref, sems.at[1])
    dims_copy.start()
    wave_copy.start()
    dims_copy.wait()
    lines = lax.broadcasted_iota(jnp.int32, (8, 128), 0)
    facts = jnp.where(lines == 1, dims_ref[0, 0], jnp.where(lines == 2, dims_ref[0, 1], 0)).astype(jnp.float32)
    wave_copy.wait()
    held = jnp.where(live(facts, wave_ref.shape), wave_ref[...], 0.0)
    u_ref[...] = (held * SCALE).astype(jnp.bfloat16)
    facts_ref[...] = jnp.where(lines == 0, total(held * held), facts)


def near_kernel(width, rows, self_ref, near_ref, far_ref, left_hbm, right_hbm, out_ref, left_ref, right_ref, sems):
    offsets, _ = place(1, width)
    copies = []
    at = 0
    for n, (offset, count) in enumerate([(0, 2)] + [(o, width) for o in offsets[: 2 + rows]]):
        pair = []
        for e, (source, target) in enumerate(((right_hbm, right_ref), (left_hbm, left_ref))):
            copy = pltpu.make_async_copy(
                source.at[0, pl.ds(offset, count)], target.at[pl.ds(at, count)], sems.at[n, e])
            copy.start()
            pair.append(copy)
        copies.append((pair, at, count))
        at += count
    for n, source in enumerate((self_ref, near_ref, far_ref)):
        pair, first, count = copies[n]
        for copy in pair:
            copy.wait()
        out_ref[n] = terms(source[...], left_ref, right_ref, first, count)
    for pair, _, _ in copies[3:]:
        for copy in pair:
            copy.wait()


def first_kernel(width, rows, facts_ref, u_ref, part_ref, left_ref, right_ref, *refs):
    row_refs, (row_out_ref, image_ref, w_ref, stats_ref) = refs[:rows], refs[rows:]
    facts = facts_ref[...]
    image = part_ref[0] + part_ref[1] + part_ref[2]
    for r in range(rows):
        piece = terms(row_refs[r][...], left_ref, right_ref, 2 + (2 + r) * width, width)
        row_out_ref[r] = piece
        image = image + piece
    image = jnp.where(live(facts, image.shape), image, 0.0)
    image_ref[...] = image
    u = u_ref[...].astype(jnp.float32)
    square = total(u * u)
    cross = total(u * image)
    rho = jnp.where(square > 0.0, cross / square, 0.0)
    w = image - rho * u
    w_ref[...] = w.astype(jnp.bfloat16)
    lines = lax.broadcasted_iota(jnp.int32, (8, 128), 0)
    stats = jnp.where(lines == 0, facts, 0.0)
    for line, value in ((1, square), (2, cross), (3, total(w * w)), (4, rho)):
        stats = jnp.where(lines == line, value, stats)
    stats_ref[...] = stats


def image_kernel(width, rows, self_ref, near_ref, far_ref, left_ref, right_ref, *refs):
    row_refs, (out_ref,) = refs[:rows], refs[rows:]
    image = terms(self_ref[...], left_ref, right_ref, 0, 2)
    for n, source in enumerate((near_ref, far_ref) + row_refs):
        image = image + terms(source[...], left_ref, right_ref, 2 + n * width, width)
    out_ref[...] = image


def second_kernel(size, width, rows, cells, facts_ref, stats_ref, hw_ref, part_ref, row_part_ref, image_ref,
                  first_hbm, second_hbm, first_ref, second_ref, sems):
    _, partners = place(size, width)
    facts = facts_ref[...]
    stats = stats_ref[...]
    sums = jnp.sum(stats, axis=0)
    start, square, cross, inner = (sums[i : i + 1, 0:1] for i in range(4))
    scale = lax.rsqrt(start / cells + 1e-06) * (1.0 / SCALE)
    first_ref[...] = image_ref[...] * scale
    first_copy = pltpu.make_async_copy(first_ref, first_hbm.at[0], sems.at[0])
    first_copy.start()
    rho = cross / square
    gap = stats[:, 4:5, 0:1] - rho[None]
    residual = inner + jnp.sum(stats[:, 1:2, 0:1] * gap * gap, axis=0)
    second_scale = scale * lax.rsqrt(scale * scale * (residual / cells) + 1e-06)
    image = hw_ref[...]
    for n in range(3):
        image = image + (stats_ref[partners[n], 4:5, 0:1] - rho) * part_ref[n]
    for r in range(rows):
        image = image + (stats_ref[partners[3 + r], 4:5, 0:1] - rho) * row_part_ref[r]
    second_ref[...] = jnp.where(live(facts, image.shape), image, 0.0) * second_scale
    second_copy = pltpu.make_async_copy(second_ref, second_hbm.at[0], sems.at[1])
    second_copy.start()
    first_copy.wait()
    second_copy.wait()


def body(wavefunction, sector_dims, left_env, right_env):
    size = lax.axis_size("sector")
    block = wavefunction.shape[1]
    square = (block, block)
    width = (right_env.shape[1] - 2) // 4
    near, far, row_pairs = swap_pairs(size)
    rows = len(row_pairs)
    cells = float(size * block * block)
    envs = (2 + (2 + rows) * width,) + square
    f32, bf16 = jnp.float32, jnp.bfloat16

    u, facts = pl.pallas_call(
        start_kernel, out_shape=(pltpu.VMEM(square, bf16), pltpu.VMEM((8, 128), f32)),
        in_specs=[HB, HB], out_specs=(VM, VM),
        scratch_shapes=[pltpu.VMEM(square, f32), pltpu.SMEM((1, 2), jnp.int32), pltpu.SemaphoreType.DMA((2,))],
        compiler_params=PARAMS,
    )(hbm(wavefunction), hbm(sector_dims))

    row_u = [vmem(swap(u, "sector", p)) for p in row_pairs]
    near_u = vmem(swap(u, "sector", near))
    far_u = vmem(swap(u, "sector", far))
    part, left, right = pl.pallas_call(
        functools.partial(near_kernel, width, rows),
        out_shape=(pltpu.VMEM((3,) + square, f32), pltpu.VMEM(envs, bf16), pltpu.VMEM(envs, bf16)),
        in_specs=[VM] * 3 + [HB] * 2, out_specs=(VM,) * 3,
        scratch_shapes=[pltpu.SemaphoreType.DMA((3 + rows, 2))], compiler_params=PARAMS,
    )(vmem(u), near_u, far_u, hbm(left_env), hbm(right_env))
    left, right, part, facts = vmem(left), vmem(right), vmem(part), vmem(facts)
    row_part, image, w, stats = pl.pallas_call(
        functools.partial(first_kernel, width, rows),
        out_shape=(pltpu.VMEM((rows,) + square, f32), pltpu.VMEM(square, f32), pltpu.VMEM(square, bf16),
                   pltpu.VMEM((8, 128), f32)),
        in_specs=[VM] * (5 + rows), out_specs=(VM,) * 4, compiler_params=PARAMS,
    )(facts, vmem(u), part, left, right, *row_u)

    row_w = [vmem(swap(w, "sector", p)) for p in row_pairs]
    near_w = vmem(swap(w, "sector", near))
    far_w = vmem(swap(w, "sector", far))
    stats = lax.all_gather(stats, "sector", axis=0)
    hw = pl.pallas_call(
        functools.partial(image_kernel, width, rows), out_shape=pltpu.VMEM(square, f32),
        in_specs=[VM] * (5 + rows), out_specs=VM, compiler_params=PARAMS,
    )(vmem(w), near_w, far_w, left, right, *row_w)
    return pl.pallas_call(
        functools.partial(second_kernel, size, width, rows, cells),
        out_shape=(jax.ShapeDtypeStruct((1,) + square, f32),) * 2,
        in_specs=[VM] * 6, out_specs=(HB, HB),
        scratch_shapes=[pltpu.VMEM(square, f32), pltpu.VMEM(square, f32), pltpu.SemaphoreType.DMA((2,))],
        compiler_params=PARAMS,
    )(facts, stats, vmem(hw), part, vmem(row_part), vmem(image))


def solution(mesh):
    placed = (
        P(("groups", "sector"), None, None),
        P(("groups", "sector"), None),
        P(("groups", "sector"), None, None, None),
        P(("groups", "sector"), None, None, None),
    )
    return jax.shard_map(
        body,
        mesh=mesh,
        in_specs=placed,
        out_specs=(P(("groups", "sector"), None, None), P(("groups", "sector"), None, None)),
        check_vma=False,
    )
```

time: 52 us -> 43.9 us (0.84)
  blocking collectives: 0 us -> 23 us
  local copies, waits for them, and re-layouts: 19.9 us -> 0 us
  starting transfers between devices: 18.8 us -> 11.6 us
  waiting for transfers between devices: 1.79 us -> 0.02 us
  Pallas kernels: 10.1 us -> 8.44 us
    all_gather x0 -> x1, blocking collectives: none -> 23 us  [body(): stats = lax.all_gather(stats, 'sector', axis=0)]
    unnamed x44 -> x0, local copies, waits for them, and re-layouts: 19.8 us -> none
    all_to_all x1 -> x0, starting transfers between devices: 4.22 us -> none  [body(): stats = lax.all_to_all(stats, 'sector', 0, 0, tiled=True)]
    ppermute x6, starting transfers between devices: 14.6 us -> 11.6 us  [swap(): lax.ppermute(x, axis, [(a, b) for a, b in pairs] + [(b, a) for a, b in pa...]
    all_to_all x1 -> x0, waiting for transfers between devices: 1.77 us -> none  [body(): stats = lax.all_to_all(stats, 'sector', 0, 0, tiled=True)]
    pallas_call x5, Pallas kernels: 10.1 us -> 8.44 us  [the longest x1 3.37 us: body(): pl.pallas_call(functools.partial(near_kernel, width, rows), out_shape=(pl...]
  transfers between devices with their start and end apart: 7 -> 6, of which waited for: 1 -> 0; matrix products, arithmetic and copies ran while one was open for 0% -> 0% of each run, Pallas kernels for 8% -> 8%
where the time goes in v2:
time: 43.9 us; the launch traced here: 43.7 us
  blocking collectives  23 us (52%)
  starting transfers between devices  11.6 us (26%)
  Pallas kernels  8.44 us (19%)
  between operations  0.68 us (2%)
    all_gather x1, blocking collectives, body(): stats = lax.all_gather(stats, 'sector', axis=0)  23 us
    ppermute x6, starting transfers between devices, swap(): lax.ppermute(x, axis, [(a, b) for a, b in pairs] + [(b, a) for a, b in pa...  11.6 us
    pallas_call x1, Pallas kernels, body(): pl.pallas_call(functools.partial(near_kernel, width, rows), out_shape=(pl...  3.37 us
    pallas_call x1, Pallas kernels, body(): pl.pallas_call(functools.partial(image_kernel, width, rows), out_shape=pl...  1.8 us
    pallas_call x1, Pallas kernels, body(): pl.pallas_call(start_kernel, out_shape=(pltpu.VMEM(square, bf16), pltpu.V...  1.13 us
    pallas_call x1, Pallas kernels, body(): pl.pallas_call(functools.partial(first_kernel, width, rows), out_shape=(p...  1.09 us
    pallas_call x1, Pallas kernels, body(): pl.pallas_call(functools.partial(second_kernel, size, width, rows, cells)...  1.05 us
  transfers between devices with their start and end apart: 6, of which 0 were waited for; matrix products, arithmetic and copies ran while one was open for 0% of the time, Pallas kernels for 8%

profile of v2, /device:TPU:0, one launch (start us, length us, event | category | flops | bytes accessed | tf_op | source)
XLA Modules:
  0.0 43.7 jit_solution(14193528003886132397)
XLA Ops:
  0.6 1.1 %shard_map.59 = (bf16[256,256]{1,0:T(8,128)(2,1)S(1)}, f32[8,128]{1,0:T(8,128)S(1)}) custom-call(f32[1,256,256]{2,1,0:T(8,128)} %wave_hbm.1, s32[1,2]{1,0:T(1,128)} %dims_hbm.1), custom_call_target="tpu_custom_call" | custom-call | tf_op jit(solution)/shard_map/pallas_call | solution.py:180
  1.8 0.5 %collective-permute-start = (bf16[256,256]{1,0:T(8,128)(2,1)S(1)}, bf16[256,256]{1,0:T(8,128)(2,1)S(1)}, u32[]{:S(2)}, u32[]{:S(2)}) collective-permute-start(bf16[256,256]{1,0:T(8,128)(2,1)S(1)} %get-tuple-element.12.self_ref.u_ref), channel_id=1, source_target_pairs={{0,1},{2,3},{4,5},{6,7},{8,9},{10,11},{12,13},{14,15},{1,0},{3,2},... | collective-permute-start | bytes 393224 | tf_op jit(solution)/shard_map/ppermute | solution.py:27
  2.3 0.7 %collective-permute-start.1 = (bf16[256,256]{1,0:T(8,128)(2,1)S(1)}, bf16[256,256]{1,0:T(8,128)(2,1)S(1)}, u32[]{:S(2)}, u32[]{:S(2)}) collective-permute-start(bf16[256,256]{1,0:T(8,128)(2,1)S(1)} %get-tuple-element.12.self_ref.u_ref), channel_id=1, source_target_pairs={{1,2},{3,4},{5,6},{9,10},{11,12},{13,14},{2,1},{4,3},{6,5},{10,9},... | collective-permute-start | bytes 393224 | tf_op jit(solution)/shard_map/ppermute | solution.py:27
  3.0 3.7 %collective-permute-start.2 = (bf16[256,256]{1,0:T(8,128)(2,1)S(1)}, bf16[256,256]{1,0:T(8,128)(2,1)S(1)}, u32[]{:S(2)}, u32[]{:S(2)}) collective-permute-start(bf16[256,256]{1,0:T(8,128)(2,1)S(1)} %get-tuple-element.12.self_ref.u_ref), channel_id=1, source_target_pairs={{0,8},{1,9},{2,10},{3,11},{4,12},{5,13},{6,14},{7,15},{8,0},{9,1},... | collective-permute-start | bytes 393224 | tf_op jit(solution)/shard_map/ppermute | solution.py:27
  6.6 0.0 collective-permute-done.near_ref
  6.6 0.0 collective-permute-done.1.far_ref
  6.6 3.4 %shard_map.60 = (f32[3,256,256]{2,1,0:T(8,128)S(1)}, bf16[20,256,256]{2,1,0:T(8,128)(2,1)S(1)}, bf16[20,256,256]{2,1,0:T(8,128)(2,1)S(1)}) custom-call(bf16[256,256]{1,0:T(8,128)(2,1)S(1)} %get-tuple-element.12.self_ref.u_ref, bf16[256,256]{1,0:T(8,128)(2,1)S(1)} %collective-permute-done.near_ref, bf16[256,256]{1,0:T(8,128)(2,1)S(1)} %collective-permute-done.1.far_ref, ...), custom_call_target="tpu_custom_call" | custom-call | tf_op jit(solution)/shard_map/pallas_call | solution.py:190
  10.0 0.0 collective-permute-done.2.refs_0_
  10.0 1.1 %shard_map.61 = (f32[1,256,256]{2,1,0:T(8,128)S(1)}, f32[256,256]{1,0:T(8,128)S(1)}, bf16[256,256]{1,0:T(8,128)(2,1)S(1)}, f32[8,128]{1,0:T(8,128)S(1)}) custom-call(f32[8,128]{1,0:T(8,128)S(1)} %get-tuple-element.11.facts_ref, bf16[256,256]{1,0:T(8,128)(2,1)S(1)} %get-tuple-element.12.self_ref.u_ref, f32[3,256,256]{2,1,0:T(8,128)S(1)} %get-tuple-element.13.part_ref, ...), custom_call_target="tpu_custom_call" | custom-call | tf_op jit(solution)/shard_map/pallas_call | solution.py:197
  11.1 3.1 %collective-permute-start.3 = (bf16[256,256]{1,0:T(8,128)(2,1)S(1)}, bf16[256,256]{1,0:T(8,128)(2,1)S(1)}, u32[]{:S(2)}, u32[]{:S(2)}) collective-permute-start(bf16[256,256]{1,0:T(8,128)(2,1)S(1)} %get-tuple-element.17.self_ref), channel_id=1, source_target_pairs={{0,1},{2,3},{4,5},{6,7},{8,9},{10,11},{12,13},{14,15},{1,0},{3,2},... | collective-permute-start | bytes 393224 | tf_op jit(solution)/shard_map/ppermute | solution.py:27
  14.2 0.7 %collective-permute-start.4 = (bf16[256,256]{1,0:T(8,128)(2,1)S(1)}, bf16[256,256]{1,0:T(8,128)(2,1)S(1)}, u32[]{:S(2)}, u32[]{:S(2)}) collective-permute-start(bf16[256,256]{1,0:T(8,128)(2,1)S(1)} %get-tuple-element.17.self_ref), channel_id=1, source_target_pairs={{1,2},{3,4},{5,6},{9,10},{11,12},{13,14},{2,1},{4,3},{6,5},{10,9},... | collective-permute-start | bytes 393224 | tf_op jit(solution)/shard_map/ppermute | solution.py:27
  14.8 3.0 %collective-permute-start.5 = (bf16[256,256]{1,0:T(8,128)(2,1)S(1)}, bf16[256,256]{1,0:T(8,128)(2,1)S(1)}, u32[]{:S(2)}, u32[]{:S(2)}) collective-permute-start(bf16[256,256]{1,0:T(8,128)(2,1)S(1)} %get-tuple-element.17.self_ref), channel_id=1, source_target_pairs={{0,8},{1,9},{2,10},{3,11},{4,12},{5,13},{6,14},{7,15},{8,0},{9,1},... | collective-permute-start | bytes 393224 | tf_op jit(solution)/shard_map/ppermute | solution.py:27
  17.9 23.0 %all-gather = f32[128,128]{1,0:T(8,128)S(1)} all-gather(f32[8,128]{1,0:T(8,128)S(1)} %get-tuple-element.16), channel_id=2, replica_groups=mesh['groups'=2,'sector'=16] {'sector'}, dimensions={0}, use_global_device_ids=true | all-gather | bytes 69632 | tf_op jit(solution)/shard_map/all_gather | solution.py:207
  40.8 0.0 collective-permute-done.3.near_ref
  40.8 0.0 collective-permute-done.4.far_ref
  40.8 0.0 collective-permute-done.5.refs_0_
  40.8 1.8 %shard_map.62.hw_ref = f32[256,256]{1,0:T(8,128)S(1)} custom-call(bf16[256,256]{1,0:T(8,128)(2,1)S(1)} %get-tuple-element.17.self_ref, bf16[256,256]{1,0:T(8,128)(2,1)S(1)} %collective-permute-done.3.near_ref, bf16[256,256]{1,0:T(8,128)(2,1)S(1)} %collective-permute-done.4.far_ref, bf16[20,256,256]{2,1,0:T(8,128)(2,1)S(1)} %get-tuple-element.14.left_ref, ...), custom_call_target="tpu_custom_call" | custom-call | tf_op jit(solution)/shard_map/pallas_call | solution.py:208
  42.6 1.0 %shard_map.63 = (f32[1,256,256]{2,1,0:T(8,128)}, f32[1,256,256]{2,1,0:T(8,128)}) custom-call(f32[8,128]{1,0:T(8,128)S(1)} %get-tuple-element.11.facts_ref, f32[16,8,128]{2,1,0:T(8,128)S(1)} %bitcast.1, f32[256,256]{1,0:T(8,128)S(1)} %shard_map.62.hw_ref, f32[3,256,256]{2,1,0:T(8,128)S(1)} %get-tuple-element.13.part_ref, ...), custom_call_target="tpu_custom_call" | custom-call | tf_op jit(solution)/shard_map/pallas_call | solution.py:212
Async XLA Ops:
  1.8 4.9 %collective-permute-start = (bf16[256,256]{1,0:T(8,128)(2,1)S(1)}, bf16[256,256]{1,0:T(8,128)(2,1)S(1)}, u32[]{:S(2)}, u32[]{:S(2)}) collective-permute-start(bf16[256,256]{1,0:T(8,128)(2,1)S(1)} %get-tuple-element.12.self_ref.u_ref), channel_id=1, source_target_pairs={{0,1},{2,3},{4,5},{6,7},{8,9},{10,11},{12,13},{14,15},{1,0},{3,2},... | collective-permute-start | bytes 393224 | tf_op jit(solution)/shard_map/ppermute | solution.py:27
  2.3 4.3 %collective-permute-start.1 = (bf16[256,256]{1,0:T(8,128)(2,1)S(1)}, bf16[256,256]{1,0:T(8,128)(2,1)S(1)}, u32[]{:S(2)}, u32[]{:S(2)}) collective-permute-start(bf16[256,256]{1,0:T(8,128)(2,1)S(1)} %get-tuple-element.12.self_ref.u_ref), channel_id=1, source_target_pairs={{1,2},{3,4},{5,6},{9,10},{11,12},{13,14},{2,1},{4,3},{6,5},{10,9},... | collective-permute-start | bytes 393224 | tf_op jit(solution)/shard_map/ppermute | solution.py:27
  3.0 7.1 %collective-permute-start.2 = (bf16[256,256]{1,0:T(8,128)(2,1)S(1)}, bf16[256,256]{1,0:T(8,128)(2,1)S(1)}, u32[]{:S(2)}, u32[]{:S(2)}) collective-permute-start(bf16[256,256]{1,0:T(8,128)(2,1)S(1)} %get-tuple-element.12.self_ref.u_ref), channel_id=1, source_target_pairs={{0,8},{1,9},{2,10},{3,11},{4,12},{5,13},{6,14},{7,15},{8,0},{9,1},... | collective-permute-start | bytes 393224 | tf_op jit(solution)/shard_map/ppermute | solution.py:27
  11.1 29.7 %collective-permute-start.3 = (bf16[256,256]{1,0:T(8,128)(2,1)S(1)}, bf16[256,256]{1,0:T(8,128)(2,1)S(1)}, u32[]{:S(2)}, u32[]{:S(2)}) collective-permute-start(bf16[256,256]{1,0:T(8,128)(2,1)S(1)} %get-tuple-element.17.self_ref), channel_id=1, source_target_pairs={{0,1},{2,3},{4,5},{6,7},{8,9},{10,11},{12,13},{14,15},{1,0},{3,2},... | collective-permute-start | bytes 393224 | tf_op jit(solution)/shard_map/ppermute | solution.py:27
  14.2 26.7 %collective-permute-start.4 = (bf16[256,256]{1,0:T(8,128)(2,1)S(1)}, bf16[256,256]{1,0:T(8,128)(2,1)S(1)}, u32[]{:S(2)}, u32[]{:S(2)}) collective-permute-start(bf16[256,256]{1,0:T(8,128)(2,1)S(1)} %get-tuple-element.17.self_ref), channel_id=1, source_target_pairs={{1,2},{3,4},{5,6},{9,10},{11,12},{13,14},{2,1},{4,3},{6,5},{10,9},... | collective-permute-start | bytes 393224 | tf_op jit(solution)/shard_map/ppermute | solution.py:27
  14.8 26.0 %collective-permute-start.5 = (bf16[256,256]{1,0:T(8,128)(2,1)S(1)}, bf16[256,256]{1,0:T(8,128)(2,1)S(1)}, u32[]{:S(2)}, u32[]{:S(2)}) collective-permute-start(bf16[256,256]{1,0:T(8,128)(2,1)S(1)} %get-tuple-element.17.self_ref), channel_id=1, source_target_pairs={{0,8},{1,9},{2,10},{3,11},{4,12},{5,13},{6,14},{7,15},{8,0},{9,1},... | collective-permute-start | bytes 393224 | tf_op jit(solution)/shard_map/ppermute | solution.py:27

commit v3 on v2

v3 whole, which is shorter than its diff:
```python
import functools

import jax
import jax.numpy as jnp
from jax import lax
from jax.experimental import pallas as pl
from jax.experimental.pallas import tpu as pltpu
from jax.sharding import PartitionSpec as P

QD = 8
SCALE = 1024.0
NT = (((1,), (1,)), ((), ()))
VM = pl.BlockSpec(memory_space=pltpu.VMEM)
HB = pl.BlockSpec(memory_space=pltpu.HBM)
PARAMS = pltpu.CompilerParams(vmem_limit_bytes=16 * 1024 * 1024)


def vmem(x):
    return pltpu.with_memory_space_constraint(x, pltpu.VMEM)


def hbm(x):
    return pltpu.with_memory_space_constraint(x, pltpu.HBM)


def swap(x, axis, pairs):
    to = {a: b for p in pairs for a, b in (p, p[::-1])}
    return lax.ppermute(x, axis, [(s, to.get(s, s)) for s in range(lax.axis_size(axis))])


def swap_pairs(size):
    rows = size // QD
    near = [(s, s + 1) for s in range(0, size, 2)]
    far = [(s, s + 1) for s in range(1, size - 1, 2) if s % QD != QD - 1]
    row_even = [(s, s + QD) for r in range(0, rows - 1, 2) for s in range(r * QD, r * QD + QD)]
    row_odd = [(s, s + QD) for r in range(1, rows - 1, 2) for s in range(r * QD, r * QD + QD)]
    return near, far, [p for p in (row_even, row_odd) if p]


def place(size, width):
    me = lax.axis_index("sector")
    column = lax.rem(me, QD)
    odd = lax.rem(me, 2) == 1
    row_odd = lax.rem(lax.div(me, QD), 2) == 1
    low, high, down, up = 2, 2 + width, 2 + 2 * width, 2 + 3 * width
    offsets = [jnp.where(odd, low, high), jnp.where(odd, high, low),
               jnp.where(row_odd, down, up), jnp.where(row_odd, up, down)]
    partners = [jnp.where(odd, me - 1, me + 1), jnp.where(odd, me + 1, me - 1),
                jnp.where(row_odd, me - QD, me + QD), jnp.where(row_odd, me + QD, me - QD)]
    there = [True, (column != 0) & (column != QD - 1), (partners[2] >= 0) & (partners[2] < size),
             (partners[3] >= 0) & (partners[3] < size)]
    partners = [me] + [jnp.clip(p, 0, size - 1) for p in partners]
    return offsets, partners, there


def live(facts, shape):
    row_ok = lax.broadcasted_iota(jnp.int32, shape, 0).astype(jnp.float32) < facts[1:2, 0:1]
    col_ok = lax.broadcasted_iota(jnp.int32, shape, 1).astype(jnp.float32) < facts[2:3, 0:1]
    return row_ok & col_ok


def total(x):
    return jnp.sum(jnp.sum(x, axis=0, keepdims=True), axis=1, keepdims=True)


def only(there, block):
    return block if there is True else jnp.where(there, block, jnp.zeros_like(block))


def terms(src, left_ref, right_ref, offset, count):
    size = src.shape[0]
    right = right_ref[pl.ds(offset, count)].reshape(count * size, size)
    partial_t = lax.dot_general(right, src, NT, preferred_element_type=jnp.float32).astype(jnp.bfloat16)
    image = None
    for k in range(count):
        piece = lax.dot_general(
            left_ref[offset + k], partial_t[k * size : (k + 1) * size], NT, preferred_element_type=jnp.float32
        )
        image = piece if image is None else image + piece
    return image


def fetch(left_hbm, right_hbm, left_ref, right_ref, sems, spans, first=0):
    copies = []
    at = first
    for n, (offset, count) in enumerate(spans):
        pair = [
            pltpu.make_async_copy(source.at[0, pl.ds(offset, count)], target.at[pl.ds(at, count)], sems.at[n, e])
            for e, (source, target) in enumerate(((right_hbm, right_ref), (left_hbm, left_ref)))
        ]
        for copy in pair:
            copy.start()
        copies.append(pair)
        at += count
    return copies


def start_kernel(wave_hbm, dims_hbm, u_ref, facts_ref, wave_ref, dims_ref, sems):
    wave_copy = pltpu.make_async_copy(wave_hbm.at[0], wave_ref, sems.at[0])
    dims_copy = pltpu.make_async_copy(dims_hbm, dims_ref, sems.at[1])
    dims_copy.start()
    wave_copy.start()
    dims_copy.wait()
    lines = lax.broadcasted_iota(jnp.int32, (8, 128), 0)
    facts = jnp.where(lines == 1, dims_ref[0, 0], jnp.where(lines == 2, dims_ref[0, 1], 0)).astype(jnp.float32)
    wave_copy.wait()
    held = jnp.where(live(facts, wave_ref.shape), wave_ref[...], 0.0)
    u_ref[...] = (held * SCALE).astype(jnp.bfloat16)
    facts_ref[...] = jnp.where(lines == 0, total(held * held), facts)


def near_kernel(size, width, rows, self_ref, near_ref, left_hbm, right_hbm, out_ref, left_ref, right_ref,
                left_own, right_own, sems, later_sems):
    offsets, _, _ = place(size, width)
    own = fetch(left_hbm, right_hbm, left_own, right_own, sems, [(0, 2), (offsets[0], width)])
    later = fetch(left_hbm, right_hbm, left_ref, right_ref, later_sems, [(o, width) for o in offsets[1 : 2 + rows]])
    for n, (source, first, count) in enumerate(((self_ref, 0, 2), (near_ref, 2, width))):
        for copy in own[n]:
            copy.wait()
        out_ref[n] = terms(source[...], left_own, right_own, first, count)
    for pair in later:
        for copy in pair:
            copy.wait()


def first_kernel(size, width, rows, *refs):
    part_ref, facts_ref, u_ref, left_ref, right_ref, far_ref = refs[:6]
    row_refs, (out_ref, image_ref, w_ref, stats_ref) = refs[6 : 6 + rows], refs[6 + rows :]
    _, _, there = place(size, width)
    facts = facts_ref[...]
    image = part_ref[0] + part_ref[1]
    for n, source in enumerate((far_ref,) + row_refs):
        piece = terms(only(there[1 + n], source[...]), left_ref, right_ref, n * width, width)
        out_ref[n] = piece
        image = image + piece
    image = jnp.where(live(facts, image.shape), image, 0.0)
    image_ref[...] = image
    u = u_ref[...].astype(jnp.float32)
    square = total(u * u)
    cross = total(u * image)
    rho = jnp.where(square > 0.0, cross / square, 0.0)
    w = image - rho * u
    w_ref[...] = w.astype(jnp.bfloat16)
    lines = lax.broadcasted_iota(jnp.int32, (8, 128), 0)
    stats = jnp.where(lines == 0, facts, 0.0)
    for line, value in ((1, square), (2, cross), (3, total(w * w)), (4, rho)):
        stats = jnp.where(lines == line, value, stats)
    for n in range(stats_ref.shape[0]):
        stats_ref[n] = stats


def image_kernel(size, width, rows, *refs):
    left_hbm, right_hbm, self_ref, near_ref, far_ref = refs[:5]
    row_refs, (out_ref, left_ref, right_ref, sems) = refs[5 : 5 + rows], refs[5 + rows :]
    offsets, _, there = place(size, width)
    copies = fetch(left_hbm, right_hbm, left_ref, right_ref, sems, [(0, 2)] + [(o, width) for o in offsets[: 2 + rows]])
    image = None
    at = 0
    for n, source in enumerate((self_ref, near_ref, far_ref) + row_refs):
        for copy in copies[n]:
            copy.wait()
        count = width if n else 2
        piece = terms(only(there[n - 1] if n else True, source[...]), left_ref, right_ref, at, count)
        image = piece if image is None else image + piece
        at += count
    out_ref[...] = image


def second_kernel(size, width, rows, cells, facts_ref, stats_ref, hw_ref, near_part_ref, far_part_ref, image_ref,
                  first_hbm, second_hbm, first_ref, second_ref, sems):
    _, partners, _ = place(size, width)
    facts = facts_ref[...]
    stats = stats_ref[...]
    sums = jnp.sum(stats, axis=0)
    start, square, cross, inner = (sums[i : i + 1, 0:1] for i in range(4))
    scale = lax.rsqrt(start / cells + 1e-06) * (1.0 / SCALE)
    first_ref[...] = image_ref[...] * scale
    first_copy = pltpu.make_async_copy(first_ref, first_hbm.at[0], sems.at[0])
    first_copy.start()
    rho = cross / square
    gap = stats[:, 4:5, 0:1] - rho[None]
    residual = inner + jnp.sum(stats[:, 1:2, 0:1] * gap * gap, axis=0)
    second_scale = scale * lax.rsqrt(scale * scale * (residual / cells) + 1e-06)
    image = hw_ref[...]
    for n in range(3 + rows):
        part = near_part_ref[n] if n < 2 else far_part_ref[n - 2]
        image = image + (stats_ref[partners[n], 4:5, 0:1] - rho) * part
    second_ref[...] = jnp.where(live(facts, image.shape), image, 0.0) * second_scale
    second_copy = pltpu.make_async_copy(second_ref, second_hbm.at[0], sems.at[1])
    second_copy.start()
    first_copy.wait()
    second_copy.wait()


def body(wavefunction, sector_dims, left_env, right_env):
    size = lax.axis_size("sector")
    block = wavefunction.shape[1]
    square = (block, block)
    width = (right_env.shape[1] - 2) // 4
    near, far, row_pairs = swap_pairs(size)
    rows = len(row_pairs)
    cells = float(size * block * block)
    later = ((1 + rows) * width,) + square
    own = (2 + width,) + square
    every = (2 + (2 + rows) * width,) + square
    f32, bf16 = jnp.float32, jnp.bfloat16
    dma = pltpu.SemaphoreType.DMA

    u, facts = pl.pallas_call(
        start_kernel, out_shape=(pltpu.VMEM(square, bf16), pltpu.VMEM((8, 128), f32)),
        in_specs=[HB, HB], out_specs=(VM, VM),
        scratch_shapes=[pltpu.VMEM(square, f32), pltpu.SMEM((1, 2), jnp.int32), dma((2,))],
        compiler_params=PARAMS,
    )(hbm(wavefunction), hbm(sector_dims))

    left_env, right_env = hbm(left_env), hbm(right_env)
    row_u = [vmem(swap(u, "sector", p)) for p in row_pairs]
    near_u = vmem(swap(u, "sector", near))
    far_u = vmem(swap(u, "sector", far))
    near_part, left, right = pl.pallas_call(
        functools.partial(near_kernel, size, width, rows),
        out_shape=(pltpu.VMEM((2,) + square, f32), pltpu.VMEM(later, bf16), pltpu.VMEM(later, bf16)),
        in_specs=[VM] * 2 + [HB] * 2, out_specs=(VM,) * 3,
        scratch_shapes=[pltpu.VMEM(own, bf16), pltpu.VMEM(own, bf16), dma((2, 2)), dma((1 + rows, 2))],
        compiler_params=PARAMS,
    )(vmem(u), near_u, left_env, right_env)
    near_part, facts = vmem(near_part), vmem(facts)
    far_part, image, w, stats = pl.pallas_call(
        functools.partial(first_kernel, size, width, rows),
        out_shape=(pltpu.VMEM((1 + rows,) + square, f32), pltpu.VMEM(square, f32), pltpu.VMEM(square, bf16),
                   jax.ShapeDtypeStruct((size, 8, 128), f32)),
        in_specs=[VM] * (6 + rows), out_specs=(VM,) * 4, compiler_params=PARAMS,
    )(near_part, facts, vmem(u), vmem(left), vmem(right), far_u, *row_u)

    row_w = [vmem(swap(w, "sector", p)) for p in row_pairs]
    near_w = vmem(swap(w, "sector", near))
    far_w = vmem(swap(w, "sector", far))
    stats = lax.all_to_all(stats, "sector", 0, 0, tiled=True)
    hw = pl.pallas_call(
        functools.partial(image_kernel, size, width, rows), out_shape=pltpu.VMEM(square, f32),
        in_specs=[HB] * 2 + [VM] * (3 + rows), out_specs=VM,
        scratch_shapes=[pltpu.VMEM(every, bf16), pltpu.VMEM(every, bf16), dma((3 + rows, 2))],
        compiler_params=PARAMS,
    )(left_env, right_env, vmem(w), near_w, far_w, *row_w)
    return pl.pallas_call(
        functools.partial(second_kernel, size, width, rows, cells),
        out_shape=(jax.ShapeDtypeStruct((1,) + square, f32),) * 2,
        in_specs=[VM] * 6, out_specs=(HB, HB),
        scratch_shapes=[pltpu.VMEM(square, f32), pltpu.VMEM(square, f32), dma((2,))],
        compiler_params=PARAMS,
    )(facts, stats, vmem(hw), near_part, vmem(far_part), vmem(image))


def solution(mesh):
    placed = (
        P(("groups", "sector"), None, None),
        P(("groups", "sector"), None),
        P(("groups", "sector"), None, None, None),
        P(("groups", "sector"), None, None, None),
    )
    return jax.shard_map(
        body,
        mesh=mesh,
        in_specs=placed,
        out_specs=(P(("groups", "sector"), None, None), P(("groups", "sector"), None, None)),
        check_vma=False,
    )
```

time: 43.9 us -> 32.5 us (0.74)
  blocking collectives: 23 us -> 0 us
  waiting for transfers between devices: 0.02 us -> 6.31 us
  Pallas kernels: 8.44 us -> 11.2 us
  starting transfers between devices: 11.6 us -> 14 us
    all_gather x1 -> x0, blocking collectives: 23 us -> none  [body(): stats = lax.all_gather(stats, 'sector', axis=0)]
    all_to_all x0 -> x1, starting transfers between devices: none -> 4.61 us  [body(): stats = lax.all_to_all(stats, 'sector', 0, 0, tiled=True)]
    ppermute x6, waiting for transfers between devices: 0.02 us -> 3.38 us  [swap(): lax.ppermute(x, axis, [(s, to.get(s, s)) for s in range(lax.axis_size(axi...]
    all_to_all x0 -> x1, waiting for transfers between devices: none -> 2.94 us  [body(): stats = lax.all_to_all(stats, 'sector', 0, 0, tiled=True)]
    pallas_call x3, Pallas kernels: 6.26 us -> 8.99 us  [the longest x1 3.92 us: body(): pl.pallas_call(functools.partial(image_kernel, size, width, rows), out_sh...]
    ppermute x6, starting transfers between devices: 11.6 us -> 9.43 us  [swap(): lax.ppermute(x, axis, [(s, to.get(s, s)) for s in range(lax.axis_size(axi...]
  transfers between devices with their start and end apart: 6 -> 7, of which waited for: 0 -> 2; matrix products, arithmetic and copies ran while one was open for 0% -> 0% of each run, Pallas kernels for 8% -> 21%
where the time goes in v3:
time: 32.5 us; the launch traced here: 32.2 us
  starting transfers between devices  14 us (43%)
  Pallas kernels  11.2 us (34%)
  waiting for transfers between devices  6.31 us (19%)
  between operations  0.71 us (2%)
    ppermute x6, starting transfers between devices, swap(): lax.ppermute(x, axis, [(s, to.get(s, s)) for s in range(lax.axis_size(axi...  9.43 us
    all_to_all x1, starting transfers between devices, body(): stats = lax.all_to_all(stats, 'sector', 0, 0, tiled=True)  4.61 us
    pallas_call x1, Pallas kernels, body(): pl.pallas_call(functools.partial(image_kernel, size, width, rows), out_sh...  3.92 us
    ppermute x6, waiting for transfers between devices, swap(): lax.ppermute(x, axis, [(s, to.get(s, s)) for s in range(lax.axis_size(axi...  3.38 us
    all_to_all x1, waiting for transfers between devices, body(): stats = lax.all_to_all(stats, 'sector', 0, 0, tiled=True)  2.94 us
    pallas_call x1, Pallas kernels, body(): pl.pallas_call(functools.partial(near_kernel, size, width, rows), out_sha...  2.93 us
    pallas_call x1, Pallas kernels, body(): pl.pallas_call(functools.partial(first_kernel, size, width, rows), out_sh...  2.14 us
    pallas_call x1, Pallas kernels, body(): pl.pallas_call(start_kernel, out_shape=(pltpu.VMEM(square, bf16), pltpu.V...  1.13 us
  transfers between devices with their start and end apart: 7, of which 2 were waited for; matrix products, arithmetic and copies ran while one was open for 0% of the time, Pallas kernels for 21%

profile of v3, /device:TPU:0, one launch (start us, length us, event | category | flops | bytes accessed | tf_op | source)
XLA Modules:
  0.0 32.2 jit_solution(4819971232371382431)
XLA Ops:
  0.6 1.1 %shard_map.59 = (bf16[256,256]{1,0:T(8,128)(2,1)S(1)}, f32[8,128]{1,0:T(8,128)S(1)}) custom-call(f32[1,256,256]{2,1,0:T(8,128)} %wave_hbm.1, s32[1,2]{1,0:T(1,128)} %dims_hbm.1), custom_call_target="tpu_custom_call" | custom-call | tf_op jit(solution)/shard_map/pallas_call | solution.py:209
  1.8 0.5 %collective-permute-start = (bf16[256,256]{1,0:T(8,128)(2,1)S(1)}, bf16[256,256]{1,0:T(8,128)(2,1)S(1)}, u32[]{:S(2)}, u32[]{:S(2)}) collective-permute-start(bf16[256,256]{1,0:T(8,128)(2,1)S(1)} %get-tuple-element.12.self_ref.refs_2_), channel_id=1, source_target_pairs={{0,1},{1,0},{2,3},{3,2},{4,5},{5,4},{6,7},{7,6},{8,9},{9,8},{10,11... | collective-permute-start | bytes 393224 | tf_op jit(solution)/shard_map/ppermute | solution.py:28
  2.3 3.7 %collective-permute-start.2 = (bf16[256,256]{1,0:T(8,128)(2,1)S(1)}, bf16[256,256]{1,0:T(8,128)(2,1)S(1)}, u32[]{:S(2)}, u32[]{:S(2)}) collective-permute-start(bf16[256,256]{1,0:T(8,128)(2,1)S(1)} %get-tuple-element.12.self_ref.refs_2_), channel_id=1, source_target_pairs={{0,8},{1,9},{2,10},{3,11},{4,12},{5,13},{6,14},{7,15},{8,0},{9,1},... | collective-permute-start | bytes 393224 | tf_op jit(solution)/shard_map/ppermute | solution.py:28
  6.0 0.7 %collective-permute-start.1 = (bf16[256,256]{1,0:T(8,128)(2,1)S(1)}, bf16[256,256]{1,0:T(8,128)(2,1)S(1)}, u32[]{:S(2)}, u32[]{:S(2)}) collective-permute-start(bf16[256,256]{1,0:T(8,128)(2,1)S(1)} %get-tuple-element.12.self_ref.refs_2_), channel_id=1, source_target_pairs={{0,0},{1,2},{2,1},{3,4},{4,3},{5,6},{6,5},{7,7},{8,8},{9,10},{10,9... | collective-permute-start | bytes 393224 | tf_op jit(solution)/shard_map/ppermute | solution.py:28
  6.6 0.0 collective-permute-done.near_ref
  6.6 2.9 %shard_map.60 = (f32[2,256,256]{2,1,0:T(8,128)S(1)}, bf16[12,256,256]{2,1,0:T(8,128)(2,1)S(1)}, bf16[12,256,256]{2,1,0:T(8,128)(2,1)S(1)}) custom-call(bf16[256,256]{1,0:T(8,128)(2,1)S(1)} %get-tuple-element.12.self_ref.refs_2_, bf16[256,256]{1,0:T(8,128)(2,1)S(1)} %collective-permute-done.near_ref, bf16[1,26,256,256]{3,2,1,0:T(8,128)(2,1)} %refs_0_.1, ...), custom_call_target="tpu_custom_call" | custom-call | tf_op jit(solution)/shard_map/pallas_call | solution.py:220
  9.6 3.4 %collective-permute-done.2.refs_6_ = bf16[256,256]{1,0:T(8,128)(2,1)S(1)} collective-permute-done((bf16[256,256]{1,0:T(8,128)(2,1)S(1)}, bf16[256,256]{1,0:T(8,128)(2,1)S(1)}, u32[]{:S(2)}, u32[]{:S(2)}) %collective-permute-start.2) | collective-permute-done | bytes 131104 | tf_op jit(solution)/shard_map/ppermute | solution.py:28
  12.9 0.0 collective-permute-done.1.refs_5_
  12.9 2.1 %shard_map.61 = (f32[2,256,256]{2,1,0:T(8,128)S(1)}, f32[256,256]{1,0:T(8,128)S(1)}, bf16[256,256]{1,0:T(8,128)(2,1)S(1)}, f32[16,8,128]{2,1,0:T(8,128)}) custom-call(f32[2,256,256]{2,1,0:T(8,128)S(1)} %get-tuple-element.13.refs_0_.near_part_ref, f32[8,128]{1,0:T(8,128)S(1)} %get-tuple-element.11.refs_1_.facts_ref, ...), custom_call_target="tpu_custom_call" | custom-call | tf_op jit(solution)/shard_map/pallas_call | solution.py:228
  15.1 0.0 collective-permute-start.5
  15.1 0.7 %collective-permute-start.4 = (bf16[256,256]{1,0:T(8,128)(2,1)S(1)}, bf16[256,256]{1,0:T(8,128)(2,1)S(1)}, u32[]{:S(2)}, u32[]{:S(2)}) collective-permute-start(bf16[256,256]{1,0:T(8,128)(2,1)S(1)} %get-tuple-element.17.refs_2_), channel_id=1, source_target_pairs={{0,0},{1,2},{2,1},{3,4},{4,3},{5,6},{6,5},{7,7},{8,8},{9,10},{10,9... | collective-permute-start | bytes 393224 | tf_op jit(solution)/shard_map/ppermute | solution.py:28
  15.7 3.9 %collective-permute-start.3 = (bf16[256,256]{1,0:T(8,128)(2,1)S(1)}, bf16[256,256]{1,0:T(8,128)(2,1)S(1)}, u32[]{:S(2)}, u32[]{:S(2)}) collective-permute-start(bf16[256,256]{1,0:T(8,128)(2,1)S(1)} %get-tuple-element.17.refs_2_), channel_id=1, source_target_pairs={{0,1},{1,0},{2,3},{3,2},{4,5},{5,4},{6,7},{7,6},{8,9},{9,8},{10,11... | collective-permute-start | bytes 393224 | tf_op jit(solution)/shard_map/ppermute | solution.py:28
  19.7 4.6 %all-to-all-start = ((f32[16,8,128]{2,1,0:T(8,128)}), f32[16,8,128]{2,1,0:T(8,128)S(1)}, u32[]{:S(2)}, u32[]{:S(2)}) async-start(f32[16,8,128]{2,1,0:T(8,128)} %get-tuple-element.16), calls=%async_computation | async-start | bytes 131072 | tf_op jit(solution)/shard_map/all_to_all | solution.py:238
  24.3 0.0 collective-permute-done.5.refs_5_
  24.3 0.0 collective-permute-done.4.refs_4_
  24.3 0.0 collective-permute-done.3.refs_3_
  24.3 3.9 %shard_map.62.hw_ref = f32[256,256]{1,0:T(8,128)S(1)} custom-call(bf16[1,26,256,256]{3,2,1,0:T(8,128)(2,1)} %refs_0_.1, bf16[1,26,256,256]{3,2,1,0:T(8,128)(2,1)} %refs_1_.1, bf16[256,256]{1,0:T(8,128)(2,1)S(1)} %get-tuple-element.17.refs_2_, bf16[256,256]{1,0:T(8,128)(2,1)S(1)} %collective-permute-done.3.refs_3_, ...), custom_call_target="tpu_custom_call" | custom-call | tf_op jit(solution)/shard_map/pallas_call | solution.py:239
  28.3 2.9 %all-to-all-done.stats_ref = f32[16,8,128]{2,1,0:T(8,128)S(1)} async-done(((f32[16,8,128]{2,1,0:T(8,128)}), f32[16,8,128]{2,1,0:T(8,128)S(1)}, u32[]{:S(2)}, u32[]{:S(2)}) %all-to-all-start) | async-done | bytes 65568 | tf_op jit(solution)/shard_map/all_to_all | solution.py:238
  31.2 1.0 %shard_map.63 = (f32[1,256,256]{2,1,0:T(8,128)}, f32[1,256,256]{2,1,0:T(8,128)}) custom-call(f32[8,128]{1,0:T(8,128)S(1)} %get-tuple-element.11.refs_1_.facts_ref, f32[16,8,128]{2,1,0:T(8,128)S(1)} %all-to-all-done.stats_ref, f32[256,256]{1,0:T(8,128)S(1)} %shard_map.62.hw_ref, f32[2,256,256]{2,1,0:T(8,128)S(1)} %get-tuple-element.13.refs_0_.near_part_ref, ...), custom_call_target="tpu_custom_call" | custom-call | tf_op jit(solution)/shard_map/pallas_call | solution.py:245
Async XLA Ops:
  1.8 4.8 %collective-permute-start = (bf16[256,256]{1,0:T(8,128)(2,1)S(1)}, bf16[256,256]{1,0:T(8,128)(2,1)S(1)}, u32[]{:S(2)}, u32[]{:S(2)}) collective-permute-start(bf16[256,256]{1,0:T(8,128)(2,1)S(1)} %get-tuple-element.12.self_ref.refs_2_), channel_id=1, source_target_pairs={{0,1},{1,0},{2,3},{3,2},{4,5},{5,4},{6,7},{7,6},{8,9},{9,8},{10,11... | collective-permute-start | bytes 393224 | tf_op jit(solution)/shard_map/ppermute | solution.py:28
  2.3 10.6 %collective-permute-start.2 = (bf16[256,256]{1,0:T(8,128)(2,1)S(1)}, bf16[256,256]{1,0:T(8,128)(2,1)S(1)}, u32[]{:S(2)}, u32[]{:S(2)}) collective-permute-start(bf16[256,256]{1,0:T(8,128)(2,1)S(1)} %get-tuple-element.12.self_ref.refs_2_), channel_id=1, source_target_pairs={{0,8},{1,9},{2,10},{3,11},{4,12},{5,13},{6,14},{7,15},{8,0},{9,1},... | collective-permute-start | bytes 393224 | tf_op jit(solution)/shard_map/ppermute | solution.py:28
  6.0 7.0 %collective-permute-start.1 = (bf16[256,256]{1,0:T(8,128)(2,1)S(1)}, bf16[256,256]{1,0:T(8,128)(2,1)S(1)}, u32[]{:S(2)}, u32[]{:S(2)}) collective-permute-start(bf16[256,256]{1,0:T(8,128)(2,1)S(1)} %get-tuple-element.12.self_ref.refs_2_), channel_id=1, source_target_pairs={{0,0},{1,2},{2,1},{3,4},{4,3},{5,6},{6,5},{7,7},{8,8},{9,10},{10,9... | collective-permute-start | bytes 393224 | tf_op jit(solution)/shard_map/ppermute | solution.py:28
  15.1 9.2 %collective-permute-start.5 = (bf16[256,256]{1,0:T(8,128)(2,1)S(1)}, bf16[256,256]{1,0:T(8,128)(2,1)S(1)}, u32[]{:S(2)}, u32[]{:S(2)}) collective-permute-start(bf16[256,256]{1,0:T(8,128)(2,1)S(1)} %get-tuple-element.17.refs_2_), channel_id=1, source_target_pairs={{0,8},{1,9},{2,10},{3,11},{4,12},{5,13},{6,14},{7,15},{8,0},{9,1},... | collective-permute-start | bytes 393224 | tf_op jit(solution)/shard_map/ppermute | solution.py:28
  15.1 9.2 %collective-permute-start.4 = (bf16[256,256]{1,0:T(8,128)(2,1)S(1)}, bf16[256,256]{1,0:T(8,128)(2,1)S(1)}, u32[]{:S(2)}, u32[]{:S(2)}) collective-permute-start(bf16[256,256]{1,0:T(8,128)(2,1)S(1)} %get-tuple-element.17.refs_2_), channel_id=1, source_target_pairs={{0,0},{1,2},{2,1},{3,4},{4,3},{5,6},{6,5},{7,7},{8,8},{9,10},{10,9... | collective-permute-start | bytes 393224 | tf_op jit(solution)/shard_map/ppermute | solution.py:28
  15.7 8.6 %collective-permute-start.3 = (bf16[256,256]{1,0:T(8,128)(2,1)S(1)}, bf16[256,256]{1,0:T(8,128)(2,1)S(1)}, u32[]{:S(2)}, u32[]{:S(2)}) collective-permute-start(bf16[256,256]{1,0:T(8,128)(2,1)S(1)} %get-tuple-element.17.refs_2_), channel_id=1, source_target_pairs={{0,1},{1,0},{2,3},{3,2},{4,5},{5,4},{6,7},{7,6},{8,9},{9,8},{10,11... | collective-permute-start | bytes 393224 | tf_op jit(solution)/shard_map/ppermute | solution.py:28
  19.7 11.5 %all-to-all-start = ((f32[16,8,128]{2,1,0:T(8,128)}), f32[16,8,128]{2,1,0:T(8,128)S(1)}, u32[]{:S(2)}, u32[]{:S(2)}) async-start(f32[16,8,128]{2,1,0:T(8,128)} %get-tuple-element.16), calls=%async_computation | async-start | bytes 131072 | tf_op jit(solution)/shard_map/all_to_all | solution.py:238

commit v4 on v3

v4 whole, which is shorter than its diff:
```python
import functools

import jax
import jax.numpy as jnp
from jax import lax
from jax.experimental import pallas as pl
from jax.experimental.pallas import tpu as pltpu
from jax.sharding import PartitionSpec as P

QD = 8
SCALE = 1024.0
NT = (((1,), (1,)), ((), ()))
VM = pl.BlockSpec(memory_space=pltpu.VMEM)
HB = pl.BlockSpec(memory_space=pltpu.HBM)
AN = pl.BlockSpec(memory_space=pl.ANY)
COST = pl.CostEstimate(flops=1, bytes_accessed=1, transcendentals=0)
LONG = pl.CostEstimate(flops=4000000000, bytes_accessed=1, transcendentals=0)
PARAMS = pltpu.CompilerParams(vmem_limit_bytes=16 * 1024 * 1024)


def vmem(x):
    return pltpu.with_memory_space_constraint(x, pltpu.VMEM)


def hbm(x):
    return pltpu.with_memory_space_constraint(x, pltpu.HBM)


def swap(x, axis, pairs):
    to = {a: b for p in pairs for a, b in (p, p[::-1])}
    return lax.ppermute(x, axis, [(s, to.get(s, s)) for s in range(lax.axis_size(axis))])


def swap_pairs(size):
    rows = size // QD
    near = [(s, s + 1) for s in range(0, size, 2)]
    far = [(s, s + 1) for s in range(1, size - 1, 2) if s % QD != QD - 1]
    row_even = [(s, s + QD) for r in range(0, rows - 1, 2) for s in range(r * QD, r * QD + QD)]
    row_odd = [(s, s + QD) for r in range(1, rows - 1, 2) for s in range(r * QD, r * QD + QD)]
    return near, far, [p for p in (row_even, row_odd) if p]


def place(size, width):
    me = lax.axis_index("sector")
    column = lax.rem(me, QD)
    odd = lax.rem(me, 2) == 1
    row_odd = lax.rem(lax.div(me, QD), 2) == 1
    low, high, down, up = 2, 2 + width, 2 + 2 * width, 2 + 3 * width
    offsets = [jnp.where(odd, low, high), jnp.where(odd, high, low),
               jnp.where(row_odd, down, up), jnp.where(row_odd, up, down)]
    partners = [jnp.where(odd, me - 1, me + 1), jnp.where(odd, me + 1, me - 1),
                jnp.where(row_odd, me - QD, me + QD), jnp.where(row_odd, me + QD, me - QD)]
    there = [True, (column != 0) & (column != QD - 1), (partners[2] >= 0) & (partners[2] < size),
             (partners[3] >= 0) & (partners[3] < size)]
    partners = [me] + [jnp.clip(p, 0, size - 1) for p in partners]
    return offsets, partners, there


def live(facts, shape):
    row_ok = lax.broadcasted_iota(jnp.int32, shape, 0).astype(jnp.float32) < facts[1:2, 0:1]
    col_ok = lax.broadcasted_iota(jnp.int32, shape, 1).astype(jnp.float32) < facts[2:3, 0:1]
    return row_ok & col_ok


def total(x):
    return jnp.sum(jnp.sum(x, axis=0, keepdims=True), axis=1, keepdims=True)


def only(there, block):
    return block if there is True else jnp.where(there, block, jnp.zeros_like(block))


def terms(src, left_ref, right_ref, offset, count):
    size = src.shape[0]
    right = right_ref[pl.ds(offset, count)].reshape(count * size, size)
    partial_t = lax.dot_general(right, src, NT, preferred_element_type=jnp.float32).astype(jnp.bfloat16)
    image = None
    for k in range(count):
        piece = lax.dot_general(
            left_ref[offset + k], partial_t[k * size : (k + 1) * size], NT, preferred_element_type=jnp.float32
        )
        image = piece if image is None else image + piece
    return image


def fetch(left_hbm, right_hbm, left_ref, right_ref, sems, spans):
    copies = []
    at = 0
    for n, (offset, count) in enumerate(spans):
        pair = [
            pltpu.make_async_copy(source.at[0, pl.ds(offset, count)], target.at[pl.ds(at, count)], sems.at[n, e])
            for e, (source, target) in enumerate(((right_hbm, right_ref), (left_hbm, left_ref)))
        ]
        for copy in pair:
            copy.start()
        copies.append(pair)
        at += count
    return copies


def start_kernel(wave_hbm, dims_hbm, u_ref, far_u_ref, facts_ref, wave_ref, dims_ref, sems):
    wave_copy = pltpu.make_async_copy(wave_hbm.at[0], wave_ref, sems.at[0])
    dims_copy = pltpu.make_async_copy(dims_hbm, dims_ref, sems.at[1])
    dims_copy.start()
    wave_copy.start()
    dims_copy.wait()
    lines = lax.broadcasted_iota(jnp.int32, (8, 128), 0)
    facts = jnp.where(lines == 1, dims_ref[0, 0], jnp.where(lines == 2, dims_ref[0, 1], 0)).astype(jnp.float32)
    wave_copy.wait()
    held = jnp.where(live(facts, wave_ref.shape), wave_ref[...], 0.0)
    u_ref[...] = (held * SCALE).astype(jnp.bfloat16)
    far_u_ref[...] = u_ref[...]
    facts_ref[...] = jnp.where(lines == 0, total(held * held), facts)


def near_kernel(size, width, rows, left_hbm, right_hbm, self_ref, near_ref, out_ref, left_ref, right_ref, sems):
    offsets, _, _ = place(size, width)
    copies = fetch(left_hbm, right_hbm, left_ref, right_ref, sems, [(0, 2)] + [(o, width) for o in offsets[: 2 + rows]])
    for n, (source, first, count) in enumerate(((self_ref, 0, 2), (near_ref, 2, width))):
        for copy in copies[n]:
            copy.wait()
        out_ref[n] = terms(source[...], left_ref, right_ref, first, count)
    for pair in copies[2:]:
        for copy in pair:
            copy.wait()


def far_kernel(size, width, left_ref, right_ref, far_ref, out_ref):
    _, _, there = place(size, width)
    out_ref[...] = terms(only(there[1], far_ref[...]), left_ref, right_ref, 2 + width, width)


def first_kernel(size, width, rows, *refs):
    near_part_ref, far_part_ref, facts_ref, u_ref, left_ref, right_ref = refs[:6]
    row_refs, (out_ref, image_ref, w_ref, far_w_ref, stats_ref) = refs[6 : 6 + rows], refs[6 + rows :]
    _, _, there = place(size, width)
    facts = facts_ref[...]
    image = near_part_ref[0] + near_part_ref[1] + far_part_ref[...]
    for r, source in enumerate(row_refs):
        piece = terms(only(there[2 + r], source[...]), left_ref, right_ref, 2 + (2 + r) * width, width)
        out_ref[r] = piece
        image = image + piece
    image = jnp.where(live(facts, image.shape), image, 0.0)
    image_ref[...] = image
    u = u_ref[...].astype(jnp.float32)
    square = total(u * u)
    cross = total(u * image)
    rho = jnp.where(square > 0.0, cross / square, 0.0)
    w = image - rho * u
    for ref in (w_ref, far_w_ref):
        ref[...] = w.astype(jnp.bfloat16)
    lane = lax.broadcasted_iota(jnp.int32, (1, 128), 1)
    record = jnp.zeros((1, 128), jnp.float32)
    for n, value in enumerate((facts[0:1, 0:1], square, cross, total(w * w), rho)):
        record = jnp.where(lane == n, value, record)
    mine = lax.broadcasted_iota(jnp.int32, stats_ref.shape, 0) == lax.axis_index("sector")
    stats_ref[...] = jnp.where(mine, record, 0.0)


def add_kernel(one_ref, other_ref, *refs):
    refs[len(refs) // 2][...] = one_ref[...] + other_ref[...]


def merge(stats, other, held=None):
    extra = [] if held is None else [held]
    out = pl.pallas_call(
        add_kernel, out_shape=[pltpu.VMEM(x.shape, x.dtype) for x in [stats] + extra],
        in_specs=[VM] * 2 + [AN] * len(extra), out_specs=[VM] + [AN] * len(extra),
        input_output_aliases={2: 1} if extra else {}, compiler_params=PARAMS, cost_estimate=COST,
    )(vmem(stats), vmem(other), *map(vmem, extra))
    return out


def pass_kernel(*refs):
    pass


def after(held, first):
    return pl.pallas_call(
        pass_kernel, out_shape=pltpu.VMEM(held.shape, held.dtype), in_specs=[AN] * 2, out_specs=AN,
        input_output_aliases={0: 0}, compiler_params=PARAMS, cost_estimate=COST,
    )(vmem(held), vmem(first))


def image_kernel(size, width, rows, *refs):
    left_ref, right_ref, self_ref, near_ref, far_ref = refs[:5]
    row_refs, (out_ref,) = refs[5 : 5 + rows], refs[5 + rows :]
    _, _, there = place(size, width)
    image = terms(self_ref[...], left_ref, right_ref, 0, 2)
    for n, source in enumerate((near_ref, far_ref) + row_refs):
        image = image + terms(only(there[n], source[...]), left_ref, right_ref, 2 + n * width, width)
    out_ref[...] = image


def second_kernel(size, width, rows, cells, facts_ref, stats_ref, other_stats_ref, hw_ref, near_part_ref, far_part_ref,
                  row_part_ref, image_ref, first_hbm, second_hbm, first_ref, second_ref, sems):
    _, partners, _ = place(size, width)
    facts = facts_ref[...]
    stats = stats_ref[...] + other_stats_ref[...]
    sums = jnp.sum(stats, axis=0, keepdims=True)
    start, square, cross, inner = (sums[:, i : i + 1] for i in range(4))
    scale = lax.rsqrt(start / cells + 1e-06) * (1.0 / SCALE)
    first_ref[...] = image_ref[...] * scale
    first_copy = pltpu.make_async_copy(first_ref, first_hbm.at[0], sems.at[0])
    first_copy.start()
    rho = cross / square
    gap = stats[:, 4:5] - rho
    residual = inner + jnp.sum(stats[:, 1:2] * gap * gap, axis=0, keepdims=True)
    second_scale = scale * lax.rsqrt(scale * scale * (residual / cells) + 1e-06)
    sector = lax.broadcasted_iota(jnp.int32, gap.shape, 0)
    parts = [near_part_ref[0], near_part_ref[1], far_part_ref[...]] + [row_part_ref[r] for r in range(rows)]
    image = hw_ref[...]
    for n, part in enumerate(parts):
        image = image + jnp.sum(jnp.where(sector == partners[n], gap, 0.0), axis=0, keepdims=True) * part
    second_ref[...] = jnp.where(live(facts, image.shape), image, 0.0) * second_scale
    second_copy = pltpu.make_async_copy(second_ref, second_hbm.at[0], sems.at[1])
    second_copy.start()
    first_copy.wait()
    second_copy.wait()


def body(wavefunction, sector_dims, left_env, right_env):
    size = lax.axis_size("sector")
    block = wavefunction.shape[1]
    square = (block, block)
    width = (right_env.shape[1] - 2) // 4
    near, far, row_pairs = swap_pairs(size)
    rows = len(row_pairs)
    cells = float(size * block * block)
    every = (2 + (2 + rows) * width,) + square
    f32, bf16 = jnp.float32, jnp.bfloat16
    dma = pltpu.SemaphoreType.DMA

    u, far_u, facts = pl.pallas_call(
        start_kernel, out_shape=(pltpu.VMEM(square, bf16), pltpu.VMEM(square, bf16), pltpu.VMEM((8, 128), f32)),
        in_specs=[HB, HB], out_specs=(VM,) * 3,
        scratch_shapes=[pltpu.VMEM(square, f32), pltpu.SMEM((1, 2), jnp.int32), dma((2,))],
        compiler_params=PARAMS, cost_estimate=COST,
    )(hbm(wavefunction), hbm(sector_dims))

    left_env, right_env = hbm(left_env), hbm(right_env)
    row_u = [vmem(swap(u, "sector", p)) for p in row_pairs]
    near_u = vmem(swap(u, "sector", near))
    far_u = vmem(swap(after(far_u, near_u), "sector", far))
    near_part, left, right = pl.pallas_call(
        functools.partial(near_kernel, size, width, rows),
        out_shape=(pltpu.VMEM((2,) + square, f32), pltpu.VMEM(every, bf16), pltpu.VMEM(every, bf16)),
        in_specs=[HB] * 2 + [VM] * 2, out_specs=(VM,) * 3, scratch_shapes=[dma((3 + rows, 2))],
        compiler_params=PARAMS, cost_estimate=LONG,
    )(left_env, right_env, vmem(u), near_u)
    near_part, facts, left, right = vmem(near_part), vmem(facts), vmem(left), vmem(right)
    far_part = vmem(pl.pallas_call(
        functools.partial(far_kernel, size, width), out_shape=pltpu.VMEM(square, f32),
        in_specs=[VM] * 3, out_specs=VM, compiler_params=PARAMS, cost_estimate=LONG,
    )(left, right, far_u))
    row_part, image, w, far_w, stats = pl.pallas_call(
        functools.partial(first_kernel, size, width, rows),
        out_shape=(pltpu.VMEM((rows,) + square, f32), pltpu.VMEM(square, f32)) + (pltpu.VMEM(square, bf16),) * 2
        + (pltpu.VMEM((size, 128), f32),),
        in_specs=[VM] * (6 + rows), out_specs=(VM,) * 5, compiler_params=PARAMS, cost_estimate=COST,
    )(near_part, far_part, facts, vmem(u), left, right, *row_u)

    row_w = [vmem(swap(w, "sector", p)) for p in row_pairs]
    near_w = vmem(swap(w, "sector", near))
    step = 1
    while 2 * step < size:
        other = swap(stats, "sector", [(s, s + step) for s in range(size) if not s & step])
        if step == 1:
            stats, far_w = merge(stats, other, far_w)
        else:
            (stats,) = merge(stats, other)
        step *= 2
    other = swap(stats, "sector", [(s, s + step) for s in range(size) if not s & step])
    far_w = vmem(swap(far_w, "sector", far))
    hw = pl.pallas_call(
        functools.partial(image_kernel, size, width, rows), out_shape=pltpu.VMEM(square, f32),
        in_specs=[VM] * (5 + rows), out_specs=VM, compiler_params=PARAMS, cost_estimate=COST,
    )(left, right, vmem(w), near_w, far_w, *row_w)
    return pl.pallas_call(
        functools.partial(second_kernel, size, width, rows, cells),
        out_shape=(jax.ShapeDtypeStruct((1,) + square, f32),) * 2,
        in_specs=[VM] * 8, out_specs=(HB, HB),
        scratch_shapes=[pltpu.VMEM(square, f32), pltpu.VMEM(square, f32), dma((2,))],
        compiler_params=PARAMS, cost_estimate=COST,
    )(facts, vmem(stats), vmem(other), vmem(hw), near_part, far_part, vmem(row_part), vmem(image))


def solution(mesh):
    placed = (
        P(("groups", "sector"), None, None),
        P(("groups", "sector"), None),
        P(("groups", "sector"), None, None, None),
        P(("groups", "sector"), None, None, None),
    )
    return jax.shard_map(
        body,
        mesh=mesh,
        in_specs=placed,
        out_specs=(P(("groups", "sector"), None, None), P(("groups", "sector"), None, None)),
        check_vma=False,
    )
```

time: 32.5 us -> 36.6 us (1.13)
  waiting for transfers between devices: 6.31 us -> 10.2 us
  starting transfers between devices: 14 us -> 16.8 us
  Pallas kernels: 11.2 us -> 8.72 us
    ppermute x6 -> x10, starting transfers between devices: 9.43 us -> 16.8 us  [swap(): lax.ppermute(x, axis, [(s, to.get(s, s)) for s in range(lax.axis_size(axi...]
    ppermute x6 -> x10, waiting for transfers between devices: 3.38 us -> 10.2 us  [swap(): lax.ppermute(x, axis, [(s, to.get(s, s)) for s in range(lax.axis_size(axi...]
    all_to_all x1 -> x0, starting transfers between devices: 4.61 us -> none  [body(): stats = lax.all_to_all(stats, 'sector', 0, 0, tiled=True)]
    all_to_all x1 -> x0, waiting for transfers between devices: 2.94 us -> none  [body(): stats = lax.all_to_all(stats, 'sector', 0, 0, tiled=True)]
    pallas_call x1, Pallas kernels: 3.92 us -> 1.8 us  [body(): pl.pallas_call(functools.partial(image_kernel, size, width, rows), out_sh...]
    pallas_call x1, Pallas kernels: 2.14 us -> 1.1 us  [body(): pl.pallas_call(functools.partial(first_kernel, size, width, rows), out_sh...]
    pallas_call x0 -> x5, Pallas kernels: none -> 0.86 us  [the longest x1 0.85 us: body(): pl.pallas_call(functools.partial(far_kernel, size, width), out_shape=pltp...]
    pallas_call x1, Pallas kernels: 2.93 us -> 2.56 us  [body(): pl.pallas_call(functools.partial(near_kernel, size, width, rows), out_sha...]
  transfers between devices with their start and end apart: 7 -> 10, of which waited for: 2 -> 4; matrix products, arithmetic and copies ran while one was open for 0% -> 0% of each run, Pallas kernels for 21% -> 14%
where the time goes in v4:
time: 36.6 us; the launch traced here: 36.4 us
  starting transfers between devices  16.8 us (46%)
  waiting for transfers between devices  10.2 us (28%)
  Pallas kernels  8.72 us (24%)
  between operations  0.71 us (2%)
    ppermute x10, starting transfers between devices, swap(): lax.ppermute(x, axis, [(s, to.get(s, s)) for s in range(lax.axis_size(axi...  16.8 us
    ppermute x10, waiting for transfers between devices, swap(): lax.ppermute(x, axis, [(s, to.get(s, s)) for s in range(lax.axis_size(axi...  10.2 us
    pallas_call x1, Pallas kernels, body(): pl.pallas_call(functools.partial(near_kernel, size, width, rows), out_sha...  2.56 us
    pallas_call x1, Pallas kernels, body(): pl.pallas_call(functools.partial(image_kernel, size, width, rows), out_sh...  1.8 us
    pallas_call x1, Pallas kernels, body(): pl.pallas_call(functools.partial(second_kernel, size, width, rows, cells)...  1.27 us
    pallas_call x1, Pallas kernels, body(): pl.pallas_call(start_kernel, out_shape=(pltpu.VMEM(square, bf16), pltpu.V...  1.14 us
    pallas_call x1, Pallas kernels, body(): pl.pallas_call(functools.partial(first_kernel, size, width, rows), out_sh...  1.1 us
    pallas_call x1, Pallas kernels, body(): pl.pallas_call(functools.partial(far_kernel, size, width), out_shape=pltp...  0.85 us
  transfers between devices with their start and end apart: 10, of which 4 were waited for; matrix products, arithmetic and copies ran while one was open for 0% of the time, Pallas kernels for 14%

profile of v4, /device:TPU:0, one launch (start us, length us, event | category | flops | bytes accessed | tf_op | source)
XLA Modules:
  0.0 36.4 jit_solution(5828889785062332437)
XLA Ops:
  0.6 1.1 %shard_map.59 = (bf16[256,256]{1,0:T(8,128)(2,1)S(1)}, bf16[256,256]{1,0:T(8,128)(2,1)S(1)}, f32[8,128]{1,0:T(8,128)S(1)}) custom-call(f32[1,256,256]{2,1,0:T(8,128)} %wave_hbm.1, s32[1,2]{1,0:T(1,128)} %dims_hbm.1), custom_call_target="tpu_custom_call" | custom-call | flops 1 | bytes 1 | tf_op jit(solution)/shard_map/pallas_call | solution.py:234
  1.8 0.5 %collective-permute-start = (bf16[256,256]{1,0:T(8,128)(2,1)S(1)}, bf16[256,256]{1,0:T(8,128)(2,1)S(1)}, u32[]{:S(2)}, u32[]{:S(2)}) collective-permute-start(bf16[256,256]{1,0:T(8,128)(2,1)S(1)} %get-tuple-element.16.self_ref.refs_3_), channel_id=1, source_target_pairs={{0,1},{1,0},{2,3},{3,2},{4,5},{5,4},{6,7},{7,6},{8,9},{9,8},{10,11... | collective-permute-start | bytes 393224 | tf_op jit(solution)/shard_map/ppermute | solution.py:31
  2.3 3.7 %collective-permute-start.2 = (bf16[256,256]{1,0:T(8,128)(2,1)S(1)}, bf16[256,256]{1,0:T(8,128)(2,1)S(1)}, u32[]{:S(2)}, u32[]{:S(2)}) collective-permute-start(bf16[256,256]{1,0:T(8,128)(2,1)S(1)} %get-tuple-element.16.self_ref.refs_3_), channel_id=1, source_target_pairs={{0,8},{1,9},{2,10},{3,11},{4,12},{5,13},{6,14},{7,15},{8,0},{9,1},... | collective-permute-start | bytes 393224 | tf_op jit(solution)/shard_map/ppermute | solution.py:31
  6.0 0.0 collective-permute-done.near_ref.refs_1_
  6.0 0.7 %collective-permute-start.1 = (bf16[256,256]{1,0:T(8,128)(2,1)S(1)}, bf16[256,256]{1,0:T(8,128)(2,1)S(1)}, u32[]{:S(2)}, u32[]{:S(2)}) collective-permute-start(bf16[256,256]{1,0:T(8,128)(2,1)S(1)} %shard_map.61), channel_id=1, source_target_pairs={{0,0},{1,2},{2,1},{3,4},{4,3},{5,6},{6,5},{7,7},{8,8},{9,10},{10,9... | collective-permute-start | bytes 393224 | tf_op jit(solution)/shard_map/ppermute | solution.py:31
  6.6 2.6 %shard_map.60 = (f32[2,256,256]{2,1,0:T(8,128)S(1)}, bf16[20,256,256]{2,1,0:T(8,128)(2,1)S(1)}, bf16[20,256,256]{2,1,0:T(8,128)(2,1)S(1)}) custom-call(bf16[1,26,256,256]{3,2,1,0:T(8,128)(2,1)} %left_hbm.1, bf16[1,26,256,256]{3,2,1,0:T(8,128)(2,1)} %right_hbm.1, bf16[256,256]{1,0:T(8,128)(2,1)S(1)} %get-tuple-element.16.self_ref.refs_3_, ...), custom_call_target="tpu_custom_call" | custom-call | flops 4000000000 | bytes 1 | tf_op jit(solution)/shard_map/pallas_call | solution.py:245
  9.2 0.0 collective-permute-done.1.far_ref
  9.2 0.8 %shard_map.62.refs_1_.far_part_ref = f32[256,256]{1,0:T(8,128)S(1)} custom-call(bf16[20,256,256]{2,1,0:T(8,128)(2,1)S(1)} %get-tuple-element.18.left_ref.refs_4_.refs_0_, bf16[20,256,256]{2,1,0:T(8,128)(2,1)S(1)} %get-tuple-element.19.right_ref.refs_5_.refs_1_, bf16[256,256]{1,0:T(8,128)(2,1)S(1)} %collective-permute-done.1.far_ref), custom_call_target="tpu_custom_call" | custom-call | flops 4000000000 | bytes 1 | tf_op jit(solution)/shard_map/pallas_call | solution.py:252
  10.1 2.9 %collective-permute-done.2.refs_6_ = bf16[256,256]{1,0:T(8,128)(2,1)S(1)} collective-permute-done((bf16[256,256]{1,0:T(8,128)(2,1)S(1)}, bf16[256,256]{1,0:T(8,128)(2,1)S(1)}, u32[]{:S(2)}, u32[]{:S(2)}) %collective-permute-start.2) | collective-permute-done | bytes 131104 | tf_op jit(solution)/shard_map/ppermute | solution.py:31
  12.9 1.1 %shard_map.63 = (f32[1,256,256]{2,1,0:T(8,128)S(1)}, f32[256,256]{1,0:T(8,128)S(1)}, bf16[256,256]{1,0:T(8,128)(2,1)S(1)}, bf16[256,256]{1,0:T(8,128)(2,1)S(1)}, f32[16,128]{1,0:T(8,128)S(1)}) custom-call(f32[2,256,256]{2,1,0:T(8,128)S(1)} %get-tuple-element.17.refs_0_.near_part_ref, f32[256,256]{1,0:T(8,128)S(1)} %shard_map.62.refs_1_.far_part_ref, ...), custom_call_target="tpu_custom_call" | custom-call | flops 1 | bytes 1 | tf_op jit(solution)/shard_map/pallas_call | solution.py:256
  14.0 0.7 %collective-permute-start.3 = (f32[16,128]{1,0:T(8,128)S(1)}, f32[16,128]{1,0:T(8,128)S(1)}, u32[]{:S(2)}, u32[]{:S(2)}) collective-permute-start(f32[16,128]{1,0:T(8,128)S(1)} %get-tuple-element.21.one_ref), channel_id=1, source_target_pairs={{0,1},{1,0},{2,3},{3,2},{4,5},{5,4},{6,7},{7,6},{8,9},{9,8},{10,11... | collective-permute-start | bytes 24584 | tf_op jit(solution)/shard_map/ppermute | solution.py:31
  14.7 0.1 collective-permute-start.7
  14.8 1.0 %collective-permute-start.9 = (bf16[256,256]{1,0:T(8,128)(2,1)S(1)}, bf16[256,256]{1,0:T(8,128)(2,1)S(1)}, u32[]{:S(2)}, u32[]{:S(2)}) collective-permute-start(bf16[256,256]{1,0:T(8,128)(2,1)S(1)} %get-tuple-element.24.refs_2_), channel_id=1, source_target_pairs={{0,8},{1,9},{2,10},{3,11},{4,12},{5,13},{6,14},{7,15},{8,0},{9,1},... | collective-permute-start | bytes 393224 | tf_op jit(solution)/shard_map/ppermute | solution.py:31
  15.7 0.0 collective-permute-done.3.other_ref
  15.7 0.7 %collective-permute-start.8 = (bf16[256,256]{1,0:T(8,128)(2,1)S(1)}, bf16[256,256]{1,0:T(8,128)(2,1)S(1)}, u32[]{:S(2)}, u32[]{:S(2)}) collective-permute-start(bf16[256,256]{1,0:T(8,128)(2,1)S(1)} %get-tuple-element.25), channel_id=1, source_target_pairs={{0,0},{1,2},{2,1},{3,4},{4,3},{5,6},{6,5},{7,7},{8,8},{9,10},{10,9... | collective-permute-start | bytes 393224 | tf_op jit(solution)/shard_map/ppermute | solution.py:31
  16.4 4.6 %collective-permute-start.4 = (f32[16,128]{1,0:T(8,128)S(1)}, f32[16,128]{1,0:T(8,128)S(1)}, u32[]{:S(2)}, u32[]{:S(2)}) collective-permute-start(f32[16,128]{1,0:T(8,128)S(1)} %get-tuple-element.23.one_ref), channel_id=1, source_target_pairs={{0,2},{1,3},{2,0},{3,1},{4,6},{5,7},{6,4},{7,5},{8,10},{9,11},{10,... | collective-permute-start | bytes 24584 | tf_op jit(solution)/shard_map/ppermute | solution.py:31
  20.9 2.9 %collective-permute-done.4.other_ref = f32[16,128]{1,0:T(8,128)S(1)} collective-permute-done((f32[16,128]{1,0:T(8,128)S(1)}, f32[16,128]{1,0:T(8,128)S(1)}, u32[]{:S(2)}, u32[]{:S(2)}) %collective-permute-start.4) | collective-permute-done | bytes 8224 | tf_op jit(solution)/shard_map/ppermute | solution.py:31
  23.9 5.1 %collective-permute-start.5 = (f32[16,128]{1,0:T(8,128)S(1)}, f32[16,128]{1,0:T(8,128)S(1)}, u32[]{:S(2)}, u32[]{:S(2)}) collective-permute-start(f32[16,128]{1,0:T(8,128)S(1)} %shard_map.65.one_ref), channel_id=1, source_target_pairs={{0,4},{1,5},{2,6},{3,7},{4,0},{5,1},{6,2},{7,3},{8,12},{9,13},{10,... | collective-permute-start | bytes 24584 | tf_op jit(solution)/shard_map/ppermute | solution.py:31
  28.9 1.6 %collective-permute-done.5.other_ref = f32[16,128]{1,0:T(8,128)S(1)} collective-permute-done((f32[16,128]{1,0:T(8,128)S(1)}, f32[16,128]{1,0:T(8,128)S(1)}, u32[]{:S(2)}, u32[]{:S(2)}) %collective-permute-start.5) | collective-permute-done | bytes 8224 | tf_op jit(solution)/shard_map/ppermute | solution.py:31
  30.6 0.0 collective-permute-start.6
  30.6 0.0 collective-permute-done.7.refs_3_
  30.6 1.8 %shard_map.67.hw_ref = f32[256,256]{1,0:T(8,128)S(1)} custom-call(bf16[20,256,256]{2,1,0:T(8,128)(2,1)S(1)} %get-tuple-element.18.left_ref.refs_4_.refs_0_, bf16[20,256,256]{2,1,0:T(8,128)(2,1)S(1)} %get-tuple-element.19.right_ref.refs_5_.refs_1_, bf16[256,256]{1,0:T(8,128)(2,1)S(1)} %get-tuple-element.24.refs_2_, ...), custom_call_target="tpu_custom_call" | custom-call | flops 1 | bytes 1 | tf_op jit(solution)/shard_map/pallas_call | solution.py:275
  32.4 2.7 %collective-permute-done.6.other_stats_ref = f32[16,128]{1,0:T(8,128)S(1)} collective-permute-done((f32[16,128]{1,0:T(8,128)S(1)}, f32[16,128]{1,0:T(8,128)S(1)}, u32[]{:S(2)}, u32[]{:S(2)}) %collective-permute-start.6) | collective-permute-done | bytes 8224 | tf_op jit(solution)/shard_map/ppermute | solution.py:31
  35.1 1.3 %shard_map.68 = (f32[1,256,256]{2,1,0:T(8,128)}, f32[1,256,256]{2,1,0:T(8,128)}) custom-call(f32[8,128]{1,0:T(8,128)S(1)} %get-tuple-element.15.refs_2_.facts_ref, f32[16,128]{1,0:T(8,128)S(1)} %shard_map.66.stats_ref, f32[16,128]{1,0:T(8,128)S(1)} %collective-permute-done.6.other_stats_ref, f32[256,256]{1,0:T(8,128)S(1)} %shard_map.67.hw_ref, ...), custom_call_target="tpu_custom_call" | custom-call | flops 1 | bytes 1 | tf_op jit(solution)/shard_map/pallas_call | solution.py:279
  (6 shorter events, 0.0 us)
Async XLA Ops:
  1.8 4.2 %collective-permute-start = (bf16[256,256]{1,0:T(8,128)(2,1)S(1)}, bf16[256,256]{1,0:T(8,128)(2,1)S(1)}, u32[]{:S(2)}, u32[]{:S(2)}) collective-permute-start(bf16[256,256]{1,0:T(8,128)(2,1)S(1)} %get-tuple-element.16.self_ref.refs_3_), channel_id=1, source_target_pairs={{0,1},{1,0},{2,3},{3,2},{4,5},{5,4},{6,7},{7,6},{8,9},{9,8},{10,11... | collective-permute-start | bytes 393224 | tf_op jit(solution)/shard_map/ppermute | solution.py:31
  2.3 10.6 %collective-permute-start.2 = (bf16[256,256]{1,0:T(8,128)(2,1)S(1)}, bf16[256,256]{1,0:T(8,128)(2,1)S(1)}, u32[]{:S(2)}, u32[]{:S(2)}) collective-permute-start(bf16[256,256]{1,0:T(8,128)(2,1)S(1)} %get-tuple-element.16.self_ref.refs_3_), channel_id=1, source_target_pairs={{0,8},{1,9},{2,10},{3,11},{4,12},{5,13},{6,14},{7,15},{8,0},{9,1},... | collective-permute-start | bytes 393224 | tf_op jit(solution)/shard_map/ppermute | solution.py:31
  6.0 3.2 %collective-permute-start.1 = (bf16[256,256]{1,0:T(8,128)(2,1)S(1)}, bf16[256,256]{1,0:T(8,128)(2,1)S(1)}, u32[]{:S(2)}, u32[]{:S(2)}) collective-permute-start(bf16[256,256]{1,0:T(8,128)(2,1)S(1)} %shard_map.61), channel_id=1, source_target_pairs={{0,0},{1,2},{2,1},{3,4},{4,3},{5,6},{6,5},{7,7},{8,8},{9,10},{10,9... | collective-permute-start | bytes 393224 | tf_op jit(solution)/shard_map/ppermute | solution.py:31
  14.0 1.7 %collective-permute-start.3 = (f32[16,128]{1,0:T(8,128)S(1)}, f32[16,128]{1,0:T(8,128)S(1)}, u32[]{:S(2)}, u32[]{:S(2)}) collective-permute-start(f32[16,128]{1,0:T(8,128)S(1)} %get-tuple-element.21.one_ref), channel_id=1, source_target_pairs={{0,1},{1,0},{2,3},{3,2},{4,5},{5,4},{6,7},{7,6},{8,9},{9,8},{10,11... | collective-permute-start | bytes 24584 | tf_op jit(solution)/shard_map/ppermute | solution.py:31
  14.7 15.9 %collective-permute-start.7 = (bf16[256,256]{1,0:T(8,128)(2,1)S(1)}, bf16[256,256]{1,0:T(8,128)(2,1)S(1)}, u32[]{:S(2)}, u32[]{:S(2)}) collective-permute-start(bf16[256,256]{1,0:T(8,128)(2,1)S(1)} %get-tuple-element.24.refs_2_), channel_id=1, source_target_pairs={{0,1},{1,0},{2,3},{3,2},{4,5},{5,4},{6,7},{7,6},{8,9},{9,8},{10,11... | collective-permute-start | bytes 393224 | tf_op jit(solution)/shard_map/ppermute | solution.py:31
  14.8 15.8 %collective-permute-start.9 = (bf16[256,256]{1,0:T(8,128)(2,1)S(1)}, bf16[256,256]{1,0:T(8,128)(2,1)S(1)}, u32[]{:S(2)}, u32[]{:S(2)}) collective-permute-start(bf16[256,256]{1,0:T(8,128)(2,1)S(1)} %get-tuple-element.24.refs_2_), channel_id=1, source_target_pairs={{0,8},{1,9},{2,10},{3,11},{4,12},{5,13},{6,14},{7,15},{8,0},{9,1},... | collective-permute-start | bytes 393224 | tf_op jit(solution)/shard_map/ppermute | solution.py:31
  15.7 14.9 %collective-permute-start.8 = (bf16[256,256]{1,0:T(8,128)(2,1)S(1)}, bf16[256,256]{1,0:T(8,128)(2,1)S(1)}, u32[]{:S(2)}, u32[]{:S(2)}) collective-permute-start(bf16[256,256]{1,0:T(8,128)(2,1)S(1)} %get-tuple-element.25), channel_id=1, source_target_pairs={{0,0},{1,2},{2,1},{3,4},{4,3},{5,6},{6,5},{7,7},{8,8},{9,10},{10,9... | collective-permute-start | bytes 393224 | tf_op jit(solution)/shard_map/ppermute | solution.py:31
  16.4 7.5 %collective-permute-start.4 = (f32[16,128]{1,0:T(8,128)S(1)}, f32[16,128]{1,0:T(8,128)S(1)}, u32[]{:S(2)}, u32[]{:S(2)}) collective-permute-start(f32[16,128]{1,0:T(8,128)S(1)} %get-tuple-element.23.one_ref), channel_id=1, source_target_pairs={{0,2},{1,3},{2,0},{3,1},{4,6},{5,7},{6,4},{7,5},{8,10},{9,11},{10,... | collective-permute-start | bytes 24584 | tf_op jit(solution)/shard_map/ppermute | solution.py:31
  23.9 6.7 %collective-permute-start.5 = (f32[16,128]{1,0:T(8,128)S(1)}, f32[16,128]{1,0:T(8,128)S(1)}, u32[]{:S(2)}, u32[]{:S(2)}) collective-permute-start(f32[16,128]{1,0:T(8,128)S(1)} %shard_map.65.one_ref), channel_id=1, source_target_pairs={{0,4},{1,5},{2,6},{3,7},{4,0},{5,1},{6,2},{7,3},{8,12},{9,13},{10,... | collective-permute-start | bytes 24584 | tf_op jit(solution)/shard_map/ppermute | solution.py:31
  30.6 4.5 %collective-permute-start.6 = (f32[16,128]{1,0:T(8,128)S(1)}, f32[16,128]{1,0:T(8,128)S(1)}, u32[]{:S(2)}, u32[]{:S(2)}) collective-permute-start(f32[16,128]{1,0:T(8,128)S(1)} %shard_map.66.stats_ref), channel_id=1, source_target_pairs={{0,8},{1,9},{2,10},{3,11},{4,12},{5,13},{6,14},{7,15},{8,0},{9,1},... | collective-permute-start | bytes 24584 | tf_op jit(solution)/shard_map/ppermute | solution.py:31

commit v5 on v4

--- a/solution.py
+++ b/solution.py
@@ -113,35 +113,37 @@
     facts_ref[...] = jnp.where(lines == 0, total(held * held), facts)
 
 
-def near_kernel(size, width, rows, left_hbm, right_hbm, self_ref, near_ref, out_ref, left_ref, right_ref, sems):
+def near_kernel(size, width, rows, left_hbm, right_hbm, self_ref, near_ref, out_ref, left_far, right_far, left_row, right_row,
+                left_own, right_own, sems, far_sems, row_sems):
     offsets, _, _ = place(size, width)
-    copies = fetch(left_hbm, right_hbm, left_ref, right_ref, sems, [(0, 2)] + [(o, width) for o in offsets[: 2 + rows]])
+    own = fetch(left_hbm, right_hbm, left_own, right_own, sems, [(0, 2), (offsets[0], width)])
+    later = fetch(left_hbm, right_hbm, left_far, right_far, far_sems, [(offsets[1], width)])
+    later += fetch(left_hbm, right_hbm, left_row, right_row, row_sems, [(o, width) for o in offsets[2 : 2 + rows]])
     for n, (source, first, count) in enumerate(((self_ref, 0, 2), (near_ref, 2, width))):
-        for copy in copies[n]:
+        for copy in own[n]:
             copy.wait()
-        out_ref[n] = terms(source[...], left_ref, right_ref, first, count)
-    for pair in copies[2:]:
+        out_ref[n] = terms(source[...], left_own, right_own, first, count)
+    for pair in later:
         for copy in pair:
             copy.wait()
 
 
 def far_kernel(size, width, left_ref, right_ref, far_ref, out_ref):
     _, _, there = place(size, width)
-    out_ref[...] = terms(only(there[1], far_ref[...]), left_ref, right_ref, 2 + width, width)
+    out_ref[...] = terms(only(there[1], far_ref[...]), left_ref, right_ref, 0, width)
 
 
 def first_kernel(size, width, rows, *refs):
     near_part_ref, far_part_ref, facts_ref, u_ref, left_ref, right_ref = refs[:6]
-    row_refs, (out_ref, image_ref, w_ref, far_w_ref, stats_ref) = refs[6 : 6 + rows], refs[6 + rows :]
+    row_refs, (out_ref, w_ref, far_w_ref, stats_ref) = refs[6 : 6 + rows], refs[6 + rows :]
     _, _, there = place(size, width)
     facts = facts_ref[...]
     image = near_part_ref[0] + near_part_ref[1] + far_part_ref[...]
     for r, source in enumerate(row_refs):
-        piece = terms(only(there[2 + r], source[...]), left_ref, right_ref, 2 + (2 + r) * width, width)
+        piece = terms(only(there[2 + r], source[...]), left_ref, right_ref, r * width, width)
         out_ref[r] = piece
         image = image + piece
     image = jnp.where(live(facts, image.shape), image, 0.0)
-    image_ref[...] = image
     u = u_ref[...].astype(jnp.float32)
     square = total(u * u)
     cross = total(u * image)
@@ -153,22 +155,22 @@
     record = jnp.zeros((1, 128), jnp.float32)
     for n, value in enumerate((facts[0:1, 0:1], square, cross, total(w * w), rho)):
         record = jnp.where(lane == n, value, record)
-    mine = lax.broadcasted_iota(jnp.int32, stats_ref.shape, 0) == lax.axis_index("sector")
+    mine = lax.broadcasted_iota(jnp.int32, stats_ref.shape, 0) == lax.rem(lax.axis_index("sector"), 2)
     stats_ref[...] = jnp.where(mine, record, 0.0)
 
 
-def add_kernel(one_ref, other_ref, *refs):
-    refs[len(refs) // 2][...] = one_ref[...] + other_ref[...]
-
-
-def merge(stats, other, held=None):
-    extra = [] if held is None else [held]
-    out = pl.pallas_call(
-        add_kernel, out_shape=[pltpu.VMEM(x.shape, x.dtype) for x in [stats] + extra],
-        in_specs=[VM] * 2 + [AN] * len(extra), out_specs=[VM] + [AN] * len(extra),
-        input_output_aliases={2: 1} if extra else {}, compiler_params=PARAMS, cost_estimate=COST,
-    )(vmem(stats), vmem(other), *map(vmem, extra))
-    return out
+def merge_kernel(one_ref, other_ref, held_in, out_ref, held_out):
+    both = one_ref[...] + other_ref[...]
+    for n in range(out_ref.shape[0]):
+        out_ref[n] = both
+
+
+def merge(stats, other, copies, held):
+    return pl.pallas_call(
+        merge_kernel,
+        out_shape=(jax.ShapeDtypeStruct((copies,) + stats.shape, stats.dtype), pltpu.VMEM(held.shape, held.dtype)),
+        in_specs=[VM] * 2 + [AN], out_specs=(VM, AN), input_output_aliases={2: 1}, compiler_params=PARAMS, cost_estimate=COST,
+    )(vmem(stats), vmem(other), vmem(held))
 
 
 def pass_kernel(*refs):
@@ -182,37 +184,49 @@
     )(vmem(held), vmem(first))
 
 
-def image_kernel(size, width, rows, *refs):
-    left_ref, right_ref, self_ref, near_ref, far_ref = refs[:5]
-    row_refs, (out_ref,) = refs[5 : 5 + rows], refs[5 + rows :]
-    _, _, there = place(size, width)
-    image = terms(self_ref[...], left_ref, right_ref, 0, 2)
-    for n, source in enumerate((near_ref, far_ref) + row_refs):
-        image = image + terms(only(there[n], source[...]), left_ref, right_ref, 2 + n * width, width)
+def image_kernel(size, width, rows, left_hbm, right_hbm, left_row, right_row, self_ref, near_ref, far_ref, *refs):
+    row_refs, (out_ref, left_own, right_own, sems) = refs[:rows], refs[rows:]
+    offsets, _, there = place(size, width)
+    own = fetch(left_hbm, right_hbm, left_own, right_own, sems, [(0, 2)] + [(o, width) for o in offsets[:2]])
+    image = None
+    for r, source in enumerate(row_refs):
+        piece = terms(only(there[2 + r], source[...]), left_row, right_row, r * width, width)
+        image = piece if image is None else image + piece
+    at = 0
+    for n, source in enumerate((self_ref, near_ref, far_ref)):
+        for copy in own[n]:
+            copy.wait()
+        count = width if n else 2
+        piece = terms(only(there[n - 1] if n else True, source[...]), left_own, right_own, at, count)
+        image = piece if image is None else image + piece
+        at += count
     out_ref[...] = image
 
 
-def second_kernel(size, width, rows, cells, facts_ref, stats_ref, other_stats_ref, hw_ref, near_part_ref, far_part_ref,
-                  row_part_ref, image_ref, first_hbm, second_hbm, first_ref, second_ref, sems):
+def second_kernel(size, width, rows, cells, facts_ref, stats_ref, hw_ref, near_part_ref, far_part_ref, row_part_ref,
+                  first_hbm, second_hbm, first_ref, second_ref, sems):
     _, partners, _ = place(size, width)
     facts = facts_ref[...]
-    stats = stats_ref[...] + other_stats_ref[...]
-    sums = jnp.sum(stats, axis=0, keepdims=True)
+    stats = stats_ref[...]
+    sums = jnp.sum(jnp.sum(stats, axis=0), axis=0, keepdims=True)
     start, square, cross, inner = (sums[:, i : i + 1] for i in range(4))
     scale = lax.rsqrt(start / cells + 1e-06) * (1.0 / SCALE)
-    first_ref[...] = image_ref[...] * scale
+    parts = [near_part_ref[0], near_part_ref[1], far_part_ref[...]] + [row_part_ref[r] for r in range(rows)]
+    cell = live(facts, parts[0].shape)
+    first_ref[...] = jnp.where(cell, sum(parts[1:], parts[0]), 0.0) * scale
     first_copy = pltpu.make_async_copy(first_ref, first_hbm.at[0], sems.at[0])
     first_copy.start()
     rho = cross / square
-    gap = stats[:, 4:5] - rho
-    residual = inner + jnp.sum(stats[:, 1:2] * gap * gap, axis=0, keepdims=True)
+    gap = stats[:, :, 4:5] - rho[None]
+    residual = inner + jnp.sum(jnp.sum(stats[:, :, 1:2] * gap * gap, axis=0), axis=0, keepdims=True)
     second_scale = scale * lax.rsqrt(scale * scale * (residual / cells) + 1e-06)
-    sector = lax.broadcasted_iota(jnp.int32, gap.shape, 0)
-    parts = [near_part_ref[0], near_part_ref[1], far_part_ref[...]] + [row_part_ref[r] for r in range(rows)]
+    core = lax.broadcasted_iota(jnp.int32, gap.shape, 1)
+    sector = jnp.where(core < 2, 2 * lax.broadcasted_iota(jnp.int32, gap.shape, 0) + core, -1)
     image = hw_ref[...]
     for n, part in enumerate(parts):
-        image = image + jnp.sum(jnp.where(sector == partners[n], gap, 0.0), axis=0, keepdims=True) * part
-    second_ref[...] = jnp.where(live(facts, image.shape), image, 0.0) * second_scale
+        own_gap = jnp.sum(jnp.sum(jnp.where(sector == partners[n], gap, 0.0), axis=0), axis=0, keepdims=True)
+        image = image + own_gap * part
+    second_ref[...] = jnp.where(cell, image, 0.0) * second_scale
     second_copy = pltpu.make_async_copy(second_ref, second_hbm.at[0], sems.at[1])
     second_copy.start()
     first_copy.wait()
@@ -227,7 +241,7 @@
     near, far, row_pairs = swap_pairs(size)
     rows = len(row_pairs)
     cells = float(size * block * block)
-    every = (2 + (2 + rows) * width,) + square
+    few, every, side, last = ((n,) + square for n in (2 + width, 2 + 2 * width, width, rows * width))
     f32, bf16 = jnp.float32, jnp.bfloat16
     dma = pltpu.SemaphoreType.DMA
 
@@ -242,47 +256,44 @@
     row_u = [vmem(swap(u, "sector", p)) for p in row_pairs]
     near_u = vmem(swap(u, "sector", near))
     far_u = vmem(swap(after(far_u, near_u), "sector", far))
-    near_part, left, right = pl.pallas_call(
+    near_part, left_far, right_far, left_row, right_row = pl.pallas_call(
         functools.partial(near_kernel, size, width, rows),
-        out_shape=(pltpu.VMEM((2,) + square, f32), pltpu.VMEM(every, bf16), pltpu.VMEM(every, bf16)),
-        in_specs=[HB] * 2 + [VM] * 2, out_specs=(VM,) * 3, scratch_shapes=[dma((3 + rows, 2))],
+        out_shape=(pltpu.VMEM((2,) + square, f32),) + (pltpu.VMEM(side, bf16),) * 2 + (pltpu.VMEM(last, bf16),) * 2,
+        in_specs=[HB] * 2 + [VM] * 2, out_specs=(VM,) * 5,
+        scratch_shapes=[pltpu.VMEM(few, bf16)] * 2 + [dma((2, 2)), dma((1, 2)), dma((rows, 2))],
         compiler_params=PARAMS, cost_estimate=LONG,
     )(left_env, right_env, vmem(u), near_u)
-    near_part, facts, left, right = vmem(near_part), vmem(facts), vmem(left), vmem(right)
+    near_part, facts, left_row, right_row = vmem(near_part), vmem(facts), vmem(left_row), vmem(right_row)
     far_part = vmem(pl.pallas_call(
         functools.partial(far_kernel, size, width), out_shape=pltpu.VMEM(square, f32),
         in_specs=[VM] * 3, out_specs=VM, compiler_params=PARAMS, cost_estimate=LONG,
-    )(left, right, far_u))
-    row_part, image, w, far_w, stats = pl.pallas_call(
+    )(vmem(left_far), vmem(right_far), far_u))
+    row_part, w, far_w, stats = pl.pallas_call(
         functools.partial(first_kernel, size, width, rows),
-        out_shape=(pltpu.VMEM((rows,) + square, f32), pltpu.VMEM(square, f32)) + (pltpu.VMEM(square, bf16),) * 2
-        + (pltpu.VMEM((size, 128), f32),),
-        in_specs=[VM] * (6 + rows), out_specs=(VM,) * 5, compiler_params=PARAMS, cost_estimate=COST,
-    )(near_part, far_part, facts, vmem(u), left, right, *row_u)
+        out_shape=(pltpu.VMEM((rows,) + square, f32),) + (pltpu.VMEM(square, bf16),) * 2 + (pltpu.VMEM((8, 128), f32),),
+        in_specs=[VM] * (6 + rows), out_specs=(VM,) * 4, compiler_params=PARAMS, cost_estimate=COST,
+    )(near_part, far_part, facts, vmem(u), left_row, right_row, *row_u)
 
     row_w = [vmem(swap(w, "sector", p)) for p in row_pairs]
     near_w = vmem(swap(w, "sector", near))
-    step = 1
-    while 2 * step < size:
-        other = swap(stats, "sector", [(s, s + step) for s in range(size) if not s & step])
-        if step == 1:
-            stats, far_w = merge(stats, other, far_w)
-        else:
-            (stats,) = merge(stats, other)
-        step *= 2
-    other = swap(stats, "sector", [(s, s + step) for s in range(size) if not s & step])
+    other = swap(stats, "sector", near)
+    stats, far_w = merge(stats, other, size // 2, far_w)
     far_w = vmem(swap(far_w, "sector", far))
+    chips = [list(range(0, size, 2)), list(range(1, size, 2))]
+    stats = lax.all_to_all(stats, "sector", 0, 0, tiled=True, axis_index_groups=chips)
     hw = pl.pallas_call(
         functools.partial(image_kernel, size, width, rows), out_shape=pltpu.VMEM(square, f32),
-        in_specs=[VM] * (5 + rows), out_specs=VM, compiler_params=PARAMS, cost_estimate=COST,
-    )(left, right, vmem(w), near_w, far_w, *row_w)
+        in_specs=[HB] * 2 + [VM] * (5 + rows), out_specs=VM,
+        scratch_shapes=[pltpu.VMEM(every, bf16)] * 2 + [dma((3, 2))],
+        compiler_params=PARAMS, cost_estimate=COST,
+    )(left_env, right_env, left_row, right_row, vmem(w), near_w, far_w, *row_w)
     return pl.pallas_call(
         functools.partial(second_kernel, size, width, rows, cells),
         out_shape=(jax.ShapeDtypeStruct((1,) + square, f32),) * 2,
-        in_specs=[VM] * 8, out_specs=(HB, HB),
+        in_specs=[VM] * 6, out_specs=(HB, HB),
         scratch_shapes=[pltpu.VMEM(square, f32), pltpu.VMEM(square, f32), dma((2,))],
         compiler_params=PARAMS, cost_estimate=COST,
-    )(facts, vmem(stats), vmem(other), vmem(hw), near_part, far_part, vmem(row_part), vmem(image))
+    )(facts, stats, vmem(hw), near_part, far_part, vmem(row_part))
 
 
 def solution(mesh):

time: 36.6 us -> 34.6 us (0.945)
  waiting for transfers between devices: 10.2 us -> 6.21 us
  Pallas kernels: 8.72 us -> 11 us
    ppermute x10 -> x7, starting transfers between devices: 16.8 us -> 7.17 us  [swap(): lax.ppermute(x, axis, [(s, to.get(s, s)) for s in range(lax.axis_size(axi...]
    all_to_all x0 -> x1, starting transfers between devices: none -> 9.33 us  [body(): lax.all_to_all(stats, 'sector', 0, 0, tiled=True, axis_index_groups=chips)]
    ppermute x10 -> x7, waiting for transfers between devices: 10.2 us -> 2.75 us  [swap(): lax.ppermute(x, axis, [(s, to.get(s, s)) for s in range(lax.axis_size(axi...]
    all_to_all x0 -> x1, waiting for transfers between devices: none -> 3.46 us  [body(): lax.all_to_all(stats, 'sector', 0, 0, tiled=True, axis_index_groups=chips)]
    pallas_call x1, Pallas kernels: 1.8 us -> 3.19 us  [body(): pl.pallas_call(functools.partial(image_kernel, size, width, rows), out_sh...]
    pallas_call x3 -> x1, Pallas kernels: 0.01 us -> 0.62 us  [merge(): pl.pallas_call(merge_kernel, out_shape=(jax.ShapeDtypeStruct((copies,) +...]
  transfers between devices with their start and end apart: 10 -> 8, of which waited for: 4 -> 2; matrix products, arithmetic and copies ran while one was open for 0% -> 0% of each run, Pallas kernels for 14% -> 21%
where the time goes in v5:
time: 34.6 us; the launch traced here: 34.4 us
  starting transfers between devices  16.5 us (48%)
  Pallas kernels  11 us (32%)
  waiting for transfers between devices  6.21 us (18%)
  between operations  0.71 us (2%)
    all_to_all x1, starting transfers between devices, body(): lax.all_to_all(stats, 'sector', 0, 0, tiled=True, axis_index_groups=chips)  9.33 us
    ppermute x7, starting transfers between devices, swap(): lax.ppermute(x, axis, [(s, to.get(s, s)) for s in range(lax.axis_size(axi...  7.17 us
    all_to_all x1, waiting for transfers between devices, body(): lax.all_to_all(stats, 'sector', 0, 0, tiled=True, axis_index_groups=chips)  3.46 us
    pallas_call x1, Pallas kernels, body(): pl.pallas_call(functools.partial(image_kernel, size, width, rows), out_sh...  3.19 us
    ppermute x7, waiting for transfers between devices, swap(): lax.ppermute(x, axis, [(s, to.get(s, s)) for s in range(lax.axis_size(axi...  2.75 us
    pallas_call x1, Pallas kernels, body(): pl.pallas_call(functools.partial(near_kernel, size, width, rows), out_sha...  2.69 us
    pallas_call x1, Pallas kernels, body(): pl.pallas_call(functools.partial(second_kernel, size, width, rows, cells)...  1.36 us
    pallas_call x1, Pallas kernels, body(): pl.pallas_call(start_kernel, out_shape=(pltpu.VMEM(square, bf16), pltpu.V...  1.14 us
  transfers between devices with their start and end apart: 8, of which 2 were waited for; matrix products, arithmetic and copies ran while one was open for 0% of the time, Pallas kernels for 21%

profile of v5, /device:TPU:0, one launch (start us, length us, event | category | flops | bytes accessed | tf_op | source)
XLA Modules:
  0.0 34.4 jit_solution(396763038921530565)
XLA Ops:
  0.6 1.1 %shard_map.59 = (bf16[256,256]{1,0:T(8,128)(2,1)S(1)}, bf16[256,256]{1,0:T(8,128)(2,1)S(1)}, f32[8,128]{1,0:T(8,128)S(1)}) custom-call(f32[1,256,256]{2,1,0:T(8,128)} %wave_hbm.1, s32[1,2]{1,0:T(1,128)} %dims_hbm.1), custom_call_target="tpu_custom_call" | custom-call | flops 1 | bytes 1 | tf_op jit(solution)/shard_map/pallas_call | solution.py:248
  1.8 0.5 %collective-permute-start = (bf16[256,256]{1,0:T(8,128)(2,1)S(1)}, bf16[256,256]{1,0:T(8,128)(2,1)S(1)}, u32[]{:S(2)}, u32[]{:S(2)}) collective-permute-start(bf16[256,256]{1,0:T(8,128)(2,1)S(1)} %get-tuple-element.17.self_ref.refs_3_), channel_id=1, source_target_pairs={{0,1},{1,0},{2,3},{3,2},{4,5},{5,4},{6,7},{7,6},{8,9},{9,8},{10,11... | collective-permute-start | bytes 393224 | tf_op jit(solution)/shard_map/ppermute | solution.py:31
  2.3 3.7 %collective-permute-start.2 = (bf16[256,256]{1,0:T(8,128)(2,1)S(1)}, bf16[256,256]{1,0:T(8,128)(2,1)S(1)}, u32[]{:S(2)}, u32[]{:S(2)}) collective-permute-start(bf16[256,256]{1,0:T(8,128)(2,1)S(1)} %get-tuple-element.17.self_ref.refs_3_), channel_id=1, source_target_pairs={{0,8},{1,9},{2,10},{3,11},{4,12},{5,13},{6,14},{7,15},{8,0},{9,1},... | collective-permute-start | bytes 393224 | tf_op jit(solution)/shard_map/ppermute | solution.py:31
  6.0 0.0 collective-permute-done.near_ref.refs_1_
  6.0 0.7 %collective-permute-start.1 = (bf16[256,256]{1,0:T(8,128)(2,1)S(1)}, bf16[256,256]{1,0:T(8,128)(2,1)S(1)}, u32[]{:S(2)}, u32[]{:S(2)}) collective-permute-start(bf16[256,256]{1,0:T(8,128)(2,1)S(1)} %shard_map.61), channel_id=1, source_target_pairs={{0,0},{1,2},{2,1},{3,4},{4,3},{5,6},{6,5},{7,7},{8,8},{9,10},{10,9... | collective-permute-start | bytes 393224 | tf_op jit(solution)/shard_map/ppermute | solution.py:31
  6.6 2.7 %shard_map.60 = (f32[2,256,256]{2,1,0:T(8,128)S(1)}, bf16[6,256,256]{2,1,0:T(8,128)(2,1)S(1)}, bf16[6,256,256]{2,1,0:T(8,128)(2,1)S(1)}, bf16[6,256,256]{2,1,0:T(8,128)(2,1)S(1)}, bf16[6,256,256]{2,1,0:T(8,128)(2,1)S(1)}) custom-call(bf16[1,26,256,256]{3,2,1,0:T(8,128)(2,1)} %left_hbm.3, bf16[1,26,256,256]{3,2,1,0:T(8,128)(2,1)} %right_hbm.3, ...), custom_call_target="tpu_custom_call" | custom-call | flops 4000000000 | bytes 1 | tf_op jit(solution)/shard_map/pallas_call | solution.py:259
  9.3 0.0 collective-permute-done.1.far_ref
  9.3 0.8 %shard_map.62.refs_1_.far_part_ref = f32[256,256]{1,0:T(8,128)S(1)} custom-call(bf16[6,256,256]{2,1,0:T(8,128)(2,1)S(1)} %get-tuple-element.19.left_ref, bf16[6,256,256]{2,1,0:T(8,128)(2,1)S(1)} %get-tuple-element.20.right_ref, bf16[256,256]{1,0:T(8,128)(2,1)S(1)} %collective-permute-done.1.far_ref), custom_call_target="tpu_custom_call" | custom-call | flops 4000000000 | bytes 1 | tf_op jit(solution)/shard_map/pallas_call | solution.py:267
  10.2 2.7 %collective-permute-done.2.refs_6_ = bf16[256,256]{1,0:T(8,128)(2,1)S(1)} collective-permute-done((bf16[256,256]{1,0:T(8,128)(2,1)S(1)}, bf16[256,256]{1,0:T(8,128)(2,1)S(1)}, u32[]{:S(2)}, u32[]{:S(2)}) %collective-permute-start.2) | collective-permute-done | bytes 131104 | tf_op jit(solution)/shard_map/ppermute | solution.py:31
  12.9 1.1 %shard_map.63 = (f32[1,256,256]{2,1,0:T(8,128)S(1)}, bf16[256,256]{1,0:T(8,128)(2,1)S(1)}, bf16[256,256]{1,0:T(8,128)(2,1)S(1)}, f32[8,128]{1,0:T(8,128)S(1)}) custom-call(f32[2,256,256]{2,1,0:T(8,128)S(1)} %get-tuple-element.18.refs_0_.near_part_ref, f32[256,256]{1,0:T(8,128)S(1)} %shard_map.62.refs_1_.far_part_ref, ...), custom_call_target="tpu_custom_call" | custom-call | flops 1 | bytes 1 | tf_op jit(solution)/shard_map/pallas_call | solution.py:271
  14.0 0.7 %collective-permute-start.3 = (f32[8,128]{1,0:T(8,128)S(1)}, f32[8,128]{1,0:T(8,128)S(1)}, u32[]{:S(2)}, u32[]{:S(2)}) collective-permute-start(f32[8,128]{1,0:T(8,128)S(1)} %get-tuple-element.24.one_ref), channel_id=1, source_target_pairs={{0,1},{1,0},{2,3},{3,2},{4,5},{5,4},{6,7},{7,6},{8,9},{9,8},{10,11... | collective-permute-start | bytes 12296 | tf_op jit(solution)/shard_map/ppermute | solution.py:31
  14.7 0.1 collective-permute-start.4
  14.8 1.0 %collective-permute-start.6 = (bf16[256,256]{1,0:T(8,128)(2,1)S(1)}, bf16[256,256]{1,0:T(8,128)(2,1)S(1)}, u32[]{:S(2)}, u32[]{:S(2)}) collective-permute-start(bf16[256,256]{1,0:T(8,128)(2,1)S(1)} %get-tuple-element.27.self_ref), channel_id=1, source_target_pairs={{0,8},{1,9},{2,10},{3,11},{4,12},{5,13},{6,14},{7,15},{8,0},{9,1},... | collective-permute-start | bytes 393224 | tf_op jit(solution)/shard_map/ppermute | solution.py:31
  15.7 0.0 collective-permute-done.3.other_ref
  15.7 0.6 %shard_map.64 = (f32[8,8,128]{2,1,0:T(8,128)}, bf16[256,256]{1,0:T(8,128)(2,1)S(1)}) custom-call(f32[8,128]{1,0:T(8,128)S(1)} %get-tuple-element.24.one_ref, f32[8,128]{1,0:T(8,128)S(1)} %collective-permute-done.3.other_ref, bf16[256,256]{1,0:T(8,128)(2,1)S(1)} %get-tuple-element.25.held_in), custom_call_target="tpu_custom_call", output_to_operand_aliasing={{1}: (2, {})} | custom-call | flops 1 | bytes 1 | tf_op jit(solution)/shard_map/pallas_call | solution.py:169
  16.3 0.7 %collective-permute-start.5 = (bf16[256,256]{1,0:T(8,128)(2,1)S(1)}, bf16[256,256]{1,0:T(8,128)(2,1)S(1)}, u32[]{:S(2)}, u32[]{:S(2)}) collective-permute-start(bf16[256,256]{1,0:T(8,128)(2,1)S(1)} %get-tuple-element.28), channel_id=1, source_target_pairs={{0,0},{1,2},{2,1},{3,4},{4,3},{5,6},{6,5},{7,7},{8,8},{9,10},{10,9... | collective-permute-start | bytes 393224 | tf_op jit(solution)/shard_map/ppermute | solution.py:31
  17.0 9.3 %all-to-all-start = ((f32[8,8,128]{2,1,0:T(8,128)}), f32[8,8,128]{2,1,0:T(8,128)S(1)}, u32[]{:S(2)}, u32[]{:S(2)}) async-start(f32[8,8,128]{2,1,0:T(8,128)} %get-tuple-element.26), calls=%async_computation | async-start | bytes 65536 | tf_op jit(solution)/shard_map/all_to_all | solution.py:283
  26.3 0.0 collective-permute-done.4.near_ref
  26.3 0.0 collective-permute-done.6.refs_0_
  26.3 0.0 collective-permute-done.5.far_ref
  26.3 3.2 %shard_map.65.hw_ref = f32[256,256]{1,0:T(8,128)S(1)} custom-call(bf16[1,26,256,256]{3,2,1,0:T(8,128)(2,1)} %left_hbm.3, bf16[1,26,256,256]{3,2,1,0:T(8,128)(2,1)} %right_hbm.3, bf16[6,256,256]{2,1,0:T(8,128)(2,1)S(1)} %get-tuple-element.22.refs_4_.left_row, bf16[6,256,256]{2,1,0:T(8,128)(2,1)S(1)} %get-tuple-element.23.refs_5_.right_row, ...), custom_call_target="tpu_custom_call" | custom-call | flops 1 | bytes 1 | tf_op jit(solution)/shard_map/pallas_call | solution.py:284
  29.5 3.5 %all-to-all-done.stats_ref = f32[8,8,128]{2,1,0:T(8,128)S(1)} async-done(((f32[8,8,128]{2,1,0:T(8,128)}), f32[8,8,128]{2,1,0:T(8,128)S(1)}, u32[]{:S(2)}, u32[]{:S(2)}) %all-to-all-start) | async-done | bytes 32800 | tf_op jit(solution)/shard_map/all_to_all | solution.py:283
  33.0 1.4 %shard_map.66 = (f32[1,256,256]{2,1,0:T(8,128)}, f32[1,256,256]{2,1,0:T(8,128)}) custom-call(f32[8,128]{1,0:T(8,128)S(1)} %get-tuple-element.16.refs_2_.facts_ref, f32[8,8,128]{2,1,0:T(8,128)S(1)} %all-to-all-done.stats_ref, f32[256,256]{1,0:T(8,128)S(1)} %shard_map.65.hw_ref, f32[2,256,256]{2,1,0:T(8,128)S(1)} %get-tuple-element.18.refs_0_.near_part_ref, ...), custom_call_target="tpu_custom_call" | custom-call | flops 1 | bytes 1 | tf_op jit(solution)/shard_map/pallas_call | solution.py:290
  (1 shorter events, 0.0 us)
Async XLA Ops:
  1.8 4.2 %collective-permute-start = (bf16[256,256]{1,0:T(8,128)(2,1)S(1)}, bf16[256,256]{1,0:T(8,128)(2,1)S(1)}, u32[]{:S(2)}, u32[]{:S(2)}) collective-permute-start(bf16[256,256]{1,0:T(8,128)(2,1)S(1)} %get-tuple-element.17.self_ref.refs_3_), channel_id=1, source_target_pairs={{0,1},{1,0},{2,3},{3,2},{4,5},{5,4},{6,7},{7,6},{8,9},{9,8},{10,11... | collective-permute-start | bytes 393224 | tf_op jit(solution)/shard_map/ppermute | solution.py:31
  2.3 10.6 %collective-permute-start.2 = (bf16[256,256]{1,0:T(8,128)(2,1)S(1)}, bf16[256,256]{1,0:T(8,128)(2,1)S(1)}, u32[]{:S(2)}, u32[]{:S(2)}) collective-permute-start(bf16[256,256]{1,0:T(8,128)(2,1)S(1)} %get-tuple-element.17.self_ref.refs_3_), channel_id=1, source_target_pairs={{0,8},{1,9},{2,10},{3,11},{4,12},{5,13},{6,14},{7,15},{8,0},{9,1},... | collective-permute-start | bytes 393224 | tf_op jit(solution)/shard_map/ppermute | solution.py:31
  6.0 3.4 %collective-permute-start.1 = (bf16[256,256]{1,0:T(8,128)(2,1)S(1)}, bf16[256,256]{1,0:T(8,128)(2,1)S(1)}, u32[]{:S(2)}, u32[]{:S(2)}) collective-permute-start(bf16[256,256]{1,0:T(8,128)(2,1)S(1)} %shard_map.61), channel_id=1, source_target_pairs={{0,0},{1,2},{2,1},{3,4},{4,3},{5,6},{6,5},{7,7},{8,8},{9,10},{10,9... | collective-permute-start | bytes 393224 | tf_op jit(solution)/shard_map/ppermute | solution.py:31
  14.0 1.7 %collective-permute-start.3 = (f32[8,128]{1,0:T(8,128)S(1)}, f32[8,128]{1,0:T(8,128)S(1)}, u32[]{:S(2)}, u32[]{:S(2)}) collective-permute-start(f32[8,128]{1,0:T(8,128)S(1)} %get-tuple-element.24.one_ref), channel_id=1, source_target_pairs={{0,1},{1,0},{2,3},{3,2},{4,5},{5,4},{6,7},{7,6},{8,9},{9,8},{10,11... | collective-permute-start | bytes 12296 | tf_op jit(solution)/shard_map/ppermute | solution.py:31
  14.7 11.6 %collective-permute-start.4 = (bf16[256,256]{1,0:T(8,128)(2,1)S(1)}, bf16[256,256]{1,0:T(8,128)(2,1)S(1)}, u32[]{:S(2)}, u32[]{:S(2)}) collective-permute-start(bf16[256,256]{1,0:T(8,128)(2,1)S(1)} %get-tuple-element.27.self_ref), channel_id=1, source_target_pairs={{0,1},{1,0},{2,3},{3,2},{4,5},{5,4},{6,7},{7,6},{8,9},{9,8},{10,11... | collective-permute-start | bytes 393224 | tf_op jit(solution)/shard_map/ppermute | solution.py:31
  14.8 11.6 %collective-permute-start.6 = (bf16[256,256]{1,0:T(8,128)(2,1)S(1)}, bf16[256,256]{1,0:T(8,128)(2,1)S(1)}, u32[]{:S(2)}, u32[]{:S(2)}) collective-permute-start(bf16[256,256]{1,0:T(8,128)(2,1)S(1)} %get-tuple-element.27.self_ref), channel_id=1, source_target_pairs={{0,8},{1,9},{2,10},{3,11},{4,12},{5,13},{6,14},{7,15},{8,0},{9,1},... | collective-permute-start | bytes 393224 | tf_op jit(solution)/shard_map/ppermute | solution.py:31
  16.3 10.0 %collective-permute-start.5 = (bf16[256,256]{1,0:T(8,128)(2,1)S(1)}, bf16[256,256]{1,0:T(8,128)(2,1)S(1)}, u32[]{:S(2)}, u32[]{:S(2)}) collective-permute-start(bf16[256,256]{1,0:T(8,128)(2,1)S(1)} %get-tuple-element.28), channel_id=1, source_target_pairs={{0,0},{1,2},{2,1},{3,4},{4,3},{5,6},{6,5},{7,7},{8,8},{9,10},{10,9... | collective-permute-start | bytes 393224 | tf_op jit(solution)/shard_map/ppermute | solution.py:31
  17.0 16.0 %all-to-all-start = ((f32[8,8,128]{2,1,0:T(8,128)}), f32[8,8,128]{2,1,0:T(8,128)S(1)}, u32[]{:S(2)}, u32[]{:S(2)}) async-start(f32[8,8,128]{2,1,0:T(8,128)} %get-tuple-element.26), calls=%async_computation | async-start | bytes 65536 | tf_op jit(solution)/shard_map/all_to_all | solution.py:283
